TPU v7x, 32 devices: a whole 2x2x4 slice. The times are simulated.
32 devices in a mesh: rep: 2 (over x), fsdp: 4 (over z), ctx: 4 (over y, core).
Axes of the slice: x: 2, y: 2, z: 4, core: 2. Of those that a mesh axis runs over, the one named last changes fastest.
Arguments:
- tokens: bfloat16 [8, 1024, 768], P(('rep', 'fsdp'), 'ctx'), may hold values from -6 to 6
- norm_one_gain: bfloat16 [1, 768], P(None, ('fsdp', 'ctx')), may hold values from 0.5 to 1.5
- norm_one_bias: bfloat16 [1, 768], P(None, ('fsdp', 'ctx')), may hold values from -3 to 3
- query_key_value: bfloat16 [1, 768, 2304], P(None, ('fsdp', 'ctx')), may hold values from -0.21875 to 0.21875
- query_value_bias: bfloat16 [1, 1536], P(None, ('fsdp', 'ctx')), may hold values from -3 to 3
- attention_out: bfloat16 [1, 768, 768], P(None, ('fsdp', 'ctx')), may hold values from -0.875 to 0.875
- attention_bias: bfloat16 [1, 768], P(None, ('fsdp', 'ctx')), may hold values from -3 to 3
- norm_two_gain: bfloat16 [1, 768], P(None, ('fsdp', 'ctx')), may hold values from 0.5 to 1.5
- norm_two_bias: bfloat16 [1, 768], P(None, ('fsdp', 'ctx')), may hold values from -3 to 3
- expand_weight: bfloat16 [1, 768, 3072], P(None, ('fsdp', 'ctx')), may hold values from -0.21875 to 0.21875
- expand_bias: bfloat16 [1, 3072], P(None, ('fsdp', 'ctx')), may hold values from -3 to 3
- contract_weight: bfloat16 [1, 3072, 768], P(None, ('fsdp', 'ctx')), may hold values from -0.109375 to 0.109375
- contract_bias: bfloat16 [1, 768], P(None, ('fsdp', 'ctx')), may hold values from -3 to 3
- cotangent: bfloat16 [8, 1024, 768], P(('rep', 'fsdp'), 'ctx'), may hold values from -6 to 6
Outputs:
- block_output: bfloat16 [8, 1024, 768], P(('rep', 'fsdp'), 'ctx')
- tokens_gradient: float32 [8, 1024, 768], P(('rep', 'fsdp'), 'ctx')
- norm_one_gain_gradient: float32 [1, 768], P(None, ('fsdp', 'ctx'))
- norm_one_bias_gradient: float32 [1, 768], P(None, ('fsdp', 'ctx'))
- query_key_value_gradient: float32 [1, 768, 2304], P(None, ('fsdp', 'ctx'))
- query_value_bias_gradient: float32 [1, 1536], P(None, ('fsdp', 'ctx'))
- attention_out_gradient: float32 [1, 768, 768], P(None, ('fsdp', 'ctx'))
- attention_bias_gradient: float32 [1, 768], P(None, ('fsdp', 'ctx'))
- norm_two_gain_gradient: float32 [1, 768], P(None, ('fsdp', 'ctx'))
- norm_two_bias_gradient: float32 [1, 768], P(None, ('fsdp', 'ctx'))
- expand_weight_gradient: float32 [1, 768, 3072], P(None, ('fsdp', 'ctx'))
- expand_bias_gradient: float32 [1, 3072], P(None, ('fsdp', 'ctx'))
- contract_weight_gradient: float32 [1, 3072, 768], P(None, ('fsdp', 'ctx'))
- contract_bias_gradient: float32 [1, 768], P(None, ('fsdp', 'ctx'))
All inputs are finite; a program needn't handle non-finite values.
Results may differ from a plain program's by a relative error of at most 0.018.
Values may be sent and summed in bfloat16 or wider, within the bound.
A program may use at most 128 MiB of HBM per device.

v0:
```python
import math

import jax
import jax.numpy as jnp
from jax import lax
from jax.sharding import PartitionSpec as P

H = 12


MASKED = -1e30


def norm_apply(values, gain_row, shift_row):
    center = values - jnp.mean(values, axis=-1, keepdims=True)
    spread = jnp.mean(center * center, axis=-1, keepdims=True)
    return center * lax.rsqrt(spread + 1e-05) * gain_row + shift_row


def gelu_tanh(values):
    return jax.nn.gelu(values, approximate=True)


def split_heads(matrix):
    count = matrix.shape[0]
    return matrix.reshape(count, H // 2, 2, -1).transpose(1, 0, 2, 3)


def join_heads(matrix):
    groups, count, paired, head_size = matrix.shape
    return matrix.transpose(1, 0, 2, 3).reshape(count, groups * paired * head_size)


def scores_of(queries, key_rows, query_place):
    factor = 1.0 / math.sqrt(queries.shape[-1])
    scores = (
        jnp.einsum("qhd,khd->hqk", queries, key_rows, preferred_element_type=jnp.float32) * factor
    )
    key_place = jnp.arange(key_rows.shape[0], dtype=jnp.int32)
    allowed = key_place[None, :] <= query_place[:, None]
    return (jnp.where(allowed[None], scores, MASKED), allowed)


def head_forward(queries, key_rows, value_rows, query_place):
    scores, allowed = scores_of(queries, key_rows, query_place)
    topmost = jnp.max(scores, axis=-1, keepdims=True)
    powers = jnp.exp(scores - topmost)
    totals = jnp.sum(powers, axis=-1, keepdims=True)
    soft_weights = powers / totals
    mixture = jnp.einsum(
        "hqk,khd->qhd",
        soft_weights.astype(jnp.bfloat16),
        value_rows,
        preferred_element_type=jnp.float32,
    )
    return (mixture, (topmost + jnp.log(totals))[..., 0])


def head_backward(queries, key_rows, value_rows, upstream, logsum, query_place):
    scores, allowed = scores_of(queries, key_rows, query_place)
    soft_weights = jnp.exp(scores - logsum[..., None])
    value_grad = jnp.einsum(
        "hqk,qhd->khd",
        soft_weights.astype(jnp.bfloat16),
        upstream,
        preferred_element_type=jnp.float32,
    )
    weight_grad = jnp.einsum(
        "qhd,khd->hqk", upstream, value_rows, preferred_element_type=jnp.float32
    )
    center = jnp.sum(soft_weights * weight_grad, axis=-1, keepdims=True)
    score_grad = jnp.where(allowed[None], soft_weights * (weight_grad - center), 0.0).astype(
        jnp.bfloat16
    )
    factor = 1.0 / math.sqrt(queries.shape[-1])
    query_grad = (
        jnp.einsum("hqk,khd->qhd", score_grad, key_rows, preferred_element_type=jnp.float32)
        * factor
    )
    key_grad = (
        jnp.einsum("hqk,qhd->khd", score_grad, queries, preferred_element_type=jnp.float32) * factor
    )
    return (query_grad, key_grad, value_grad)


def attend_forward(queries, key_rows, value_rows, query_place):
    mixture, logsum = lax.map(
        lambda head_pair: head_forward(head_pair[0], head_pair[1], head_pair[2], query_place),
        (split_heads(queries), split_heads(key_rows), split_heads(value_rows)),
    )
    return (join_heads(mixture), logsum)


def attend_backward(queries, key_rows, value_rows, upstream, logsum, query_place):
    grads = lax.map(
        lambda head_pair: head_backward(
            head_pair[0], head_pair[1], head_pair[2], head_pair[3], head_pair[4], query_place
        ),
        (
            split_heads(queries),
            split_heads(key_rows),
            split_heads(value_rows),
            split_heads(upstream),
            logsum,
        ),
    )
    return (join_heads(grads[0]), join_heads(grads[1]), join_heads(grads[2]))


def fetch_forward(shards, layer_at):
    pieces = [stacked[layer_at] for stacked in shards]
    return (
        lax.all_gather(pieces[0], ("fsdp", "ctx"), axis=0, tiled=True),
        lax.all_gather(pieces[1], ("fsdp", "ctx"), axis=0, tiled=True),
        lax.all_gather(pieces[2], ("fsdp", "ctx"), axis=0, tiled=True),
        lax.all_gather(pieces[3], ("fsdp", "ctx"), axis=0, tiled=True),
        lax.all_gather(pieces[4], ("fsdp", "ctx"), axis=0, tiled=True),
        lax.all_gather(pieces[5], ("fsdp", "ctx"), axis=0, tiled=True),
        lax.all_gather(pieces[6], ("fsdp", "ctx"), axis=0, tiled=True),
        lax.all_gather(pieces[7], ("fsdp", "ctx"), axis=0, tiled=True),
        lax.all_gather(pieces[8], ("fsdp", "ctx"), axis=0, tiled=True),
        lax.all_gather(pieces[9], ("fsdp", "ctx"), axis=0, tiled=True),
        lax.all_gather(pieces[10], ("fsdp", "ctx"), axis=0, tiled=True),
        lax.all_gather(pieces[11], ("fsdp", "ctx"), axis=0, tiled=True),
    )


def fetch_backward(shards, layer_at):
    pieces = [stacked[layer_at] for stacked in shards]
    return (
        lax.all_gather(pieces[0], ("fsdp", "ctx"), axis=0, tiled=True),
        lax.all_gather(pieces[1], ("fsdp", "ctx"), axis=0, tiled=True),
        lax.all_gather(pieces[2], ("fsdp", "ctx"), axis=0, tiled=True),
        lax.all_gather(pieces[3], ("fsdp", "ctx"), axis=0, tiled=True),
        lax.all_gather(pieces[4], ("fsdp", "ctx"), axis=0, tiled=True),
        lax.all_gather(pieces[5], ("fsdp", "ctx"), axis=0, tiled=True),
        lax.all_gather(pieces[6], ("fsdp", "ctx"), axis=0, tiled=True),
        lax.all_gather(pieces[7], ("fsdp", "ctx"), axis=0, tiled=True),
        lax.all_gather(pieces[8], ("fsdp", "ctx"), axis=0, tiled=True),
        lax.all_gather(pieces[9], ("fsdp", "ctx"), axis=0, tiled=True),
        lax.all_gather(pieces[10], ("fsdp", "ctx"), axis=0, tiled=True),
        lax.all_gather(pieces[11], ("fsdp", "ctx"), axis=0, tiled=True),
    )


def settle(partial_value):
    owned_parts = (
        lax.psum_scatter(
            partial_value[0].astype(jnp.bfloat16), ("fsdp", "ctx"), scatter_dimension=0, tiled=True
        ).astype(jnp.float32),
        lax.psum_scatter(
            partial_value[1].astype(jnp.bfloat16), ("fsdp", "ctx"), scatter_dimension=0, tiled=True
        ).astype(jnp.float32),
        lax.psum_scatter(
            partial_value[2].astype(jnp.bfloat16), ("fsdp", "ctx"), scatter_dimension=0, tiled=True
        ).astype(jnp.float32),
        lax.psum_scatter(
            partial_value[3].astype(jnp.bfloat16), ("fsdp", "ctx"), scatter_dimension=0, tiled=True
        ).astype(jnp.float32),
        lax.psum_scatter(
            partial_value[4].astype(jnp.bfloat16), ("fsdp", "ctx"), scatter_dimension=0, tiled=True
        ).astype(jnp.float32),
        lax.psum_scatter(
            partial_value[5].astype(jnp.bfloat16), ("fsdp", "ctx"), scatter_dimension=0, tiled=True
        ).astype(jnp.float32),
        lax.psum_scatter(
            partial_value[6].astype(jnp.bfloat16), ("fsdp", "ctx"), scatter_dimension=0, tiled=True
        ).astype(jnp.float32),
        lax.psum_scatter(
            partial_value[7].astype(jnp.bfloat16), ("fsdp", "ctx"), scatter_dimension=0, tiled=True
        ).astype(jnp.float32),
        lax.psum_scatter(
            partial_value[8].astype(jnp.bfloat16), ("fsdp", "ctx"), scatter_dimension=0, tiled=True
        ).astype(jnp.float32),
        lax.psum_scatter(
            partial_value[9].astype(jnp.bfloat16), ("fsdp", "ctx"), scatter_dimension=0, tiled=True
        ).astype(jnp.float32),
        lax.psum_scatter(
            partial_value[10].astype(jnp.bfloat16), ("fsdp", "ctx"), scatter_dimension=0, tiled=True
        ).astype(jnp.float32),
        lax.psum_scatter(
            partial_value[11].astype(jnp.bfloat16), ("fsdp", "ctx"), scatter_dimension=0, tiled=True
        ).astype(jnp.float32),
    )
    return (
        lax.psum(owned_parts[0].astype(jnp.bfloat16), "rep").astype(jnp.float32),
        lax.psum(owned_parts[1].astype(jnp.bfloat16), "rep").astype(jnp.float32),
        lax.psum(owned_parts[2].astype(jnp.bfloat16), "rep").astype(jnp.float32),
        lax.psum(owned_parts[3].astype(jnp.bfloat16), "rep").astype(jnp.float32),
        lax.psum(owned_parts[4].astype(jnp.bfloat16), "rep").astype(jnp.float32),
        lax.psum(owned_parts[5].astype(jnp.bfloat16), "rep").astype(jnp.float32),
        lax.psum(owned_parts[6].astype(jnp.bfloat16), "rep").astype(jnp.float32),
        lax.psum(owned_parts[7].astype(jnp.bfloat16), "rep").astype(jnp.float32),
        lax.psum(owned_parts[8].astype(jnp.bfloat16), "rep").astype(jnp.float32),
        lax.psum(owned_parts[9].astype(jnp.bfloat16), "rep").astype(jnp.float32),
        lax.psum(owned_parts[10].astype(jnp.bfloat16), "rep").astype(jnp.float32),
        lax.psum(owned_parts[11].astype(jnp.bfloat16), "rep").astype(jnp.float32),
    )


def layer_forward(current, params, query_place, sequences):
    (
        g_one,
        s_one,
        w_joint,
        b_joint,
        w_attend,
        b_attend,
        g_two,
        s_two,
        w_expand,
        b_expand,
        w_contract,
        b_contract,
    ) = params
    token_count, features = current.shape
    per_seq = token_count // sequences
    normed_one = norm_apply(current, g_one.astype(jnp.float32), s_one.astype(jnp.float32)).astype(
        jnp.bfloat16
    )
    bias_row = jnp.concatenate(
        [b_joint[:features], jnp.zeros((features,), jnp.bfloat16), b_joint[features:]]
    ).astype(jnp.float32)
    joint_rows = (
        jnp.dot(normed_one, w_joint, preferred_element_type=jnp.float32) + bias_row
    ).astype(jnp.bfloat16)
    queries = joint_rows[:, :features].reshape(sequences, per_seq, features)
    key_local = joint_rows[:, features : 2 * features].reshape(sequences, per_seq, features)
    value_local = joint_rows[:, 2 * features :].reshape(sequences, per_seq, features)
    key_all, value_all = (
        lax.all_gather(key_local, "ctx", axis=1, tiled=True),
        lax.all_gather(value_local, "ctx", axis=1, tiled=True),
    )
    mixture, logsum = lax.map(
        lambda sequence_item: attend_forward(
            sequence_item[0], sequence_item[1], sequence_item[2], query_place
        ),
        (queries, key_all, value_all),
    )
    mixture = mixture.reshape(token_count, features).astype(jnp.bfloat16)
    after_attend = current + (
        jnp.dot(mixture, w_attend, preferred_element_type=jnp.float32)
        + b_attend.astype(jnp.float32)
    )
    normed_two = norm_apply(
        after_attend, g_two.astype(jnp.float32), s_two.astype(jnp.float32)
    ).astype(jnp.bfloat16)
    expanded = jnp.dot(normed_two, w_expand, preferred_element_type=jnp.float32) + b_expand.astype(
        jnp.float32
    )
    activated = gelu_tanh(expanded).astype(jnp.bfloat16)
    result_rows = after_attend + (
        jnp.dot(activated, w_contract, preferred_element_type=jnp.float32)
        + b_contract.astype(jnp.float32)
    )
    saved_rows = (
        current,
        normed_one,
        joint_rows,
        key_all,
        value_all,
        logsum,
        mixture,
        after_attend,
        normed_two,
        expanded,
        activated,
    )
    return (result_rows, saved_rows)


def layer_backward(grad_rows, saved_rows, params, query_place, sequences):
    (
        g_one,
        s_one,
        w_joint,
        b_joint,
        w_attend,
        b_attend,
        g_two,
        s_two,
        w_expand,
        b_expand,
        w_contract,
        b_contract,
    ) = params
    (
        current,
        normed_one,
        joint_rows,
        key_all,
        value_all,
        logsum,
        mixture,
        after_attend,
        normed_two,
        expanded,
        activated,
    ) = saved_rows
    token_count, features = grad_rows.shape
    per_seq = token_count // sequences
    grad_low = grad_rows.astype(jnp.bfloat16)
    grad_b_contract = jnp.sum(grad_low.astype(jnp.float32), axis=0)
    grad_w_contract = jnp.dot(activated.T, grad_low, preferred_element_type=jnp.float32)
    grad_active = jnp.dot(grad_low, w_contract.T, preferred_element_type=jnp.float32)
    unused_gelu, gelu_back = jax.vjp(gelu_tanh, expanded)
    grad_expanded = gelu_back(grad_active)[0].astype(jnp.bfloat16)
    grad_b_expand = jnp.sum(grad_expanded.astype(jnp.float32), axis=0)
    grad_w_expand = jnp.dot(normed_two.T, grad_expanded, preferred_element_type=jnp.float32)
    grad_normed_two = jnp.dot(grad_expanded, w_expand.T, preferred_element_type=jnp.float32)
    unused_two, norm_back_two = jax.vjp(
        norm_apply, after_attend, g_two.astype(jnp.float32), s_two.astype(jnp.float32)
    )
    grad_after, grad_g_two, grad_s_two = norm_back_two(grad_normed_two)
    grad_after = grad_rows + grad_after
    attend_low = grad_after.astype(jnp.bfloat16)
    grad_b_attend = jnp.sum(attend_low.astype(jnp.float32), axis=0)
    grad_w_attend = jnp.dot(mixture.T, attend_low, preferred_element_type=jnp.float32)
    grad_mixture = (
        jnp.dot(attend_low, w_attend.T, preferred_element_type=jnp.float32)
        .astype(jnp.bfloat16)
        .reshape(sequences, per_seq, features)
    )
    queries = joint_rows[:, :features].reshape(sequences, per_seq, features)
    query_grad, key_part, value_part = lax.map(
        lambda sequence_item: attend_backward(
            sequence_item[0],
            sequence_item[1],
            sequence_item[2],
            sequence_item[3],
            sequence_item[4],
            query_place,
        ),
        (queries, key_all, value_all, grad_mixture, logsum),
    )
    key_grad, value_grad = (
        lax.psum_scatter(key_part, "ctx", scatter_dimension=1, tiled=True),
        lax.psum_scatter(value_part, "ctx", scatter_dimension=1, tiled=True),
    )
    grad_joint = (
        jnp.concatenate([query_grad, key_grad, value_grad], axis=-1)
        .reshape(token_count, 3 * features)
        .astype(jnp.bfloat16)
    )
    column_sums = jnp.sum(grad_joint.astype(jnp.float32), axis=0)
    grad_b_joint = jnp.concatenate([column_sums[:features], column_sums[2 * features :]])
    grad_w_joint = jnp.dot(normed_one.T, grad_joint, preferred_element_type=jnp.float32)
    grad_normed_one = jnp.dot(grad_joint, w_joint.T, preferred_element_type=jnp.float32)
    unused_one, norm_back_one = jax.vjp(
        norm_apply, current, g_one.astype(jnp.float32), s_one.astype(jnp.float32)
    )
    grad_input, grad_g_one, grad_s_one = norm_back_one(grad_normed_one)
    partial_value = (
        grad_g_one,
        grad_s_one,
        grad_w_joint,
        grad_b_joint,
        grad_w_attend,
        grad_b_attend,
        grad_g_two,
        grad_s_two,
        grad_w_expand,
        grad_b_expand,
        grad_w_contract,
        grad_b_contract,
    )
    return (grad_after + grad_input, partial_value)


def on_device(
    tokens,
    norm_one_gain,
    norm_one_bias,
    query_key_value,
    query_value_bias,
    attention_out,
    attention_bias,
    norm_two_gain,
    norm_two_bias,
    expand_weight,
    expand_bias,
    contract_weight,
    contract_bias,
    cotangent,
):
    sequences, per_seq, features = tokens.shape
    token_count = sequences * per_seq
    query_place = lax.axis_index("ctx") * per_seq + jnp.arange(per_seq, dtype=jnp.int32)
    shards = (
        norm_one_gain,
        norm_one_bias,
        query_key_value,
        query_value_bias,
        attention_out,
        attention_bias,
        norm_two_gain,
        norm_two_bias,
        expand_weight,
        expand_bias,
        contract_weight,
        contract_bias,
    )
    layers = norm_one_gain.shape[0]
    current = tokens.reshape(token_count, features).astype(jnp.float32)
    kept_params = []
    layer_at = 0
    params = fetch_forward(shards, layer_at)
    kept_params.append(params)
    current, saved_rows = layer_forward(current, params, query_place, sequences)
    stored = [saved_rows]
    block_out = current.astype(jnp.bfloat16).reshape(sequences, per_seq, features)
    grad_rows = cotangent.reshape(token_count, features).astype(jnp.float32)
    settled = [None] * layers
    for layer_at in reversed(range(layers)):
        params = fetch_backward(shards, layer_at)
        grad_rows, partial_value = layer_backward(
            grad_rows, stored[layer_at], params, query_place, sequences
        )
        settled[layer_at] = settle(partial_value)
    stacks = [jnp.stack([settled[0][member]]) for member in range(12)]
    return (
        block_out,
        grad_rows.reshape(sequences, per_seq, features),
        stacks[0],
        stacks[1],
        stacks[2],
        stacks[3],
        stacks[4],
        stacks[5],
        stacks[6],
        stacks[7],
        stacks[8],
        stacks[9],
        stacks[10],
        stacks[11],
    )


def solution(mesh):
    in_specs = (
        P(("rep", "fsdp"), "ctx", None),
        P(None, ("fsdp", "ctx")),
        P(None, ("fsdp", "ctx")),
        P(None, ("fsdp", "ctx"), None),
        P(None, ("fsdp", "ctx")),
        P(None, ("fsdp", "ctx"), None),
        P(None, ("fsdp", "ctx")),
        P(None, ("fsdp", "ctx")),
        P(None, ("fsdp", "ctx")),
        P(None, ("fsdp", "ctx"), None),
        P(None, ("fsdp", "ctx")),
        P(None, ("fsdp", "ctx"), None),
        P(None, ("fsdp", "ctx")),
        P(("rep", "fsdp"), "ctx", None),
    )
    out_specs = (
        P(("rep", "fsdp"), "ctx", None),
        P(("rep", "fsdp"), "ctx", None),
        P(None, ("fsdp", "ctx")),
        P(None, ("fsdp", "ctx")),
        P(None, ("fsdp", "ctx"), None),
        P(None, ("fsdp", "ctx")),
        P(None, ("fsdp", "ctx"), None),
        P(None, ("fsdp", "ctx")),
        P(None, ("fsdp", "ctx")),
        P(None, ("fsdp", "ctx")),
        P(None, ("fsdp", "ctx"), None),
        P(None, ("fsdp", "ctx")),
        P(None, ("fsdp", "ctx"), None),
        P(None, ("fsdp", "ctx")),
    )
    return jax.shard_map(
        on_device, mesh=mesh, in_specs=in_specs, out_specs=out_specs, check_vma=False
    )
```

profile of v0, /device:TPU:0, one launch (start us, length us, event | category | flops | bytes accessed | tf_op | source)
XLA Modules:
  0.0 797.7 jit_solution(8612413287503119404)
XLA Ops:
  17.2 63.4 %all-reduce.17 = (bf16[1536]{0:T(1024)(128)(2,1)S(1)}, bf16[768]{0:T(1024)(128)(2,1)S(1)}, bf16[768]{0:T(1024)(128)(2,1)S(1)}, bf16[768]{0:T(1024)(128)(2,1)S(1)...) all-reduce(bf16[1536]{0:T(1024)(128)(2,1)S(1)} %dynamic-update-slic, ...), channel_id=5, replica_groups=mesh['rep'=2,'fsdp'=4,'ctx'=4] {'fsdp','ctx'}, use_global_device_ids=true, to_apply=%add.2 | all-reduce | flops 8448 | bytes 33792
  90.9 14.1 %all-gather.25.cloned.1.call-done = bf16[1024,768]{1,0:T(8,128)(2,1)} async-done(((bf16[256,768]{1,0:T(8,128)(2,1)}), bf16[1024,768]{1,0:T(8,128)(2,1)}) %all-gather.25.cloned.1.call-update) | async-done | bytes 1572880 | tf_op jit(solution)/shard_map/all_gather | solution.py:231
  107.6 19.2 %all-gather.23.cloned.1.call-done = bf16[1024,768]{1,0:T(8,128)(2,1)} async-done(((bf16[256,768]{1,0:T(8,128)(2,1)}), bf16[1024,768]{1,0:T(8,128)(2,1)}) %all-gather.23.cloned.1.call-update) | async-done | bytes 1572880 | tf_op jit(solution)/shard_map/all_gather | solution.py:232
  129.5 28.8 %while.48 = (s32[]{:T(128)}, bf16[6,256,2,64]{1,3,2,0:T(8,128)(2,1)S(1)}, f32[6,2,256]{2,1,0:T(2,128)}, bf16[6,1024,2,64]{1,3,2,0:T(8,128)(2,1)}, bf16[6,256,2,6...) while((s32[]{:T(128)}, ...), condition=%wide.region_5.6_spmd.clone, body=%wide.region_2.5_spmd.clone.sunk | while | flops 140771072 | bytes 8081509 | solution.py:87
  158.4 9.1 %all-gather.27.cloned.1.call-done = bf16[1,768,768]{2,1,0:T(8,128)(2,1)} async-done(((bf16[1,48,768]{2,1,0:T(8,128)(2,1)}), bf16[1,768,768]{2,1,0:T(8,128)(2,1)}) %all-gather.27.cloned.1.call-update) | async-done | bytes 1179664 | tf_op jit(solution)/shard_map/all_gather | solution.py:117
  169.6 52.3 %all-gather.29.cloned.1.call-done = bf16[1,768,3072]{2,1,0:T(8,128)(2,1)} async-done(((bf16[1,48,3072]{2,1,0:T(8,128)(2,1)}), bf16[1,768,3072]{2,1,0:T(8,128)(2,1)}) %all-gather.29.cloned.1.call-update) | async-done | bytes 4718608 | tf_op jit(solution)/shard_map/all_gather | solution.py:121
  221.9 5.5 fusion.84
  227.4 48.6 %all-gather.31.cloned.1.call-done = bf16[1,3072,768]{2,1,0:T(8,128)(2,1)} async-done(((bf16[1,192,768]{2,1,0:T(8,128)(2,1)}), bf16[1,3072,768]{2,1,0:T(8,128)(2,1)}) %all-gather.31.cloned.1.call-update) | async-done | bytes 4718608 | tf_op jit(solution)/shard_map/all_gather | solution.py:123
  276.0 7.5 fusion.165
  289.9 88.5 %while.49 = (s32[]{:T(128)}, bf16[6,256,2,64]{1,3,2,0:T(8,128)(2,1)}, f32[6,1024,2,64]{1,3,2,0:T(8,128)}, f32[6,1024,2,64]{1,3,2,0:T(8,128)}, bf16[6,1024,2,64]{...) while((s32[]{:T(128)}, ...), condition=%wide.region_12.13_spmd.clone, body=%wide.region_10.12_spmd.clone.sunk | while | flops 343313664 | bytes 26358908 | solution.py:95
  295.4 3.6 fusion.207
  299.0 3.7 fusion.208
  310.2 3.6 fusion.207
  313.8 3.7 fusion.208
  324.9 3.6 fusion.207
  328.5 3.7 fusion.208
  339.7 3.6 fusion.207
  343.3 3.7 fusion.208
  354.5 3.6 fusion.207
  358.1 3.7 fusion.208
  372.8 3.7 fusion.208
  381.2 4.6 convolution_convert_fusion.1
  386.9 6.5 convolution_convert_fusion
  393.5 21.7 %reduce-scatter.9.cloned.1.call-done = f32[1,256,768]{1,2,0:T(8,128)} async-done(((f32[1,1024,768]{1,2,0:T(8,128)}), f32[1,256,768]{1,2,0:T(8,128)}) %reduce-scatter.9.cloned.1.call-update) | async-done | bytes 786448 | tf_op jit(solution)/shard_map/reduce_scatter | solution.py:338
  416.3 39.5 %reduce-scatter.7.cloned.1.call-done = f32[1,256,768]{1,2,0:T(8,128)} async-done(((f32[1,1024,768]{1,2,0:T(8,128)}), f32[1,256,768]{1,2,0:T(8,128)}) %reduce-scatter.7.cloned.1.call-update) | async-done | bytes 786448 | tf_op jit(solution)/shard_map/reduce_scatter | solution.py:337
  467.3 60.2 %all-reduce.16 = (bf16[768]{0:T(1024)(128)(2,1)S(1)}, bf16[768]{0:T(1024)(128)(2,1)S(1)}, bf16[768]{0:T(1024)(128)(2,1)S(1)}, bf16[1536]{0:T(1024)(128)(2,1)S(1)...) all-reduce(bf16[768]{0:T(1024)(128)(2,1)} %copy-done.25, ...), channel_id=15, replica_groups=mesh['rep'=2,'fsdp'=4,'ctx'=4] {'fsdp','ctx'}, use_global_device_ids=true, to_apply=%add.7 | all-reduce | flops 9984 | bytes 39936
  528.0 5.0 all-reduce.18
  537.1 58.9 %reduce-scatter.15.cloned.1.call-done = bf16[48,3072]{1,0:T(8,128)(2,1)} async-done(((bf16[768,3072]{1,0:T(8,128)(2,1)}), bf16[48,3072]{1,0:T(8,128)(2,1)}) %reduce-scatter.15.cloned.1.call-update) | async-done | bytes 294928 | tf_op jit(solution)/shard_map/reduce_scatter | solution.py:172
  596.0 79.0 %reduce-scatter.17.cloned.1.call-done = bf16[192,768]{1,0:T(8,128)(2,1)} async-done(((bf16[3072,768]{1,0:T(8,128)(2,1)}), bf16[192,768]{1,0:T(8,128)(2,1)}) %reduce-scatter.17.cloned.1.call-update) | async-done | bytes 294928 | tf_op jit(solution)/shard_map/reduce_scatter | solution.py:178
  675.0 70.9 %reduce-scatter.11.cloned.1.call-done = bf16[48,2304]{1,0:T(8,128)(2,1)} async-done(((bf16[768,2304]{1,0:T(8,128)(2,1)}), bf16[48,2304]{1,0:T(8,128)(2,1)}) %reduce-scatter.11.cloned.1.call-update) | async-done | bytes 221200 | tf_op jit(solution)/shard_map/reduce_scatter | solution.py:154
  748.0 5.1 fusion.110
  753.0 31.2 %all-reduce.22.cloned.1.call-done = (bf16[1,48,2304]{2,1,0:T(8,128)(2,1)}, bf16[1,48,768]{2,1,0:T(8,128)(2,1)}, bf16[1,48,3072]{2,1,0:T(8,128)(2,1)}, bf16[1,192,768]{2,1,0:T(8,128)(2,1)}) async-done(((bf16[1,48,2304]{2,1,0:T(8,128)(2,1)}, bf16[1,48,768]{2,1,0:T(8,128)(2,1)}, bf16[1,48,3072]{2,1,0:T(8,128)(2,1)}, bf16[1,192,768]{2,1,0:T(8,128)(2,1)}), (bf16[1,48,2304]{2,1,0:T(8,128)(2,1)}, ...) | async-done | bytes 884752 | tf_op jit(solution)/shard_map/psum | solution.py:188
  (252 shorter events, 136.6 us)
Async XLA Ops:
  7.2 75.9 %all-gather.21.cloned.1.call-start = ((), (), s32[]{:S(2)}) async-start(), calls=%async_computation.12 | async-start | bytes 3760128 | tf_op jit(solution)/shard_map/all_gather | solution.py:115
  7.9 97.1 %all-gather.25.cloned.1.call-start = ((), (), s32[]{:S(2)}) async-start(), calls=%async_computation.14 | async-start | bytes 1966080 | tf_op jit(solution)/shard_map/all_gather | solution.py:231
  80.6 2.5 copy-start.26
  88.0 38.9 %all-gather.23.cloned.1.call-start = ((), (), s32[]{:S(2)}) async-start(), calls=%async_computation.13 | async-start | bytes 1966080 | tf_op jit(solution)/shard_map/all_gather | solution.py:232
  88.7 78.7 %all-gather.27.cloned.1.call-start = ((), (), s32[]{:S(2)}) async-start(), calls=%async_computation.15 | async-start | bytes 1253376 | tf_op jit(solution)/shard_map/all_gather | solution.py:117
  89.3 132.6 %all-gather.29.cloned.1.call-start = ((), (), s32[]{:S(2)}) async-start(), calls=%async_computation.16 | async-start | bytes 5013504 | tf_op jit(solution)/shard_map/all_gather | solution.py:121
  89.9 186.2 %all-gather.31.cloned.1.call-start = ((), (), s32[]{:S(2)}) async-start(), calls=%async_computation.17 | async-start | bytes 5013504 | tf_op jit(solution)/shard_map/all_gather | solution.py:123
  90.4 324.7 %reduce-scatter.9.cloned.1.call-start = ((), (), s32[]{:S(2)}) async-start(), calls=%async_computation.7 | async-start | bytes 3932160 | tf_op jit(solution)/shard_map/reduce_scatter | solution.py:338
  129.5 37.9 %copy-start = (bf16[1,256,768]{2,1,0:T(8,128)(2,1)S(1)}, bf16[1,256,768]{2,1,0:T(8,128)(2,1)}, u32[]{:S(2)}) copy-start(bf16[1,256,768]{2,1,0:T(8,128)(2,1)} %param.18) | copy-start | bytes 1179652
  158.4 9.1 %copy-start.15 = (bf16[6,256,2,64]{1,3,2,0:T(8,128)(2,1)}, bf16[6,256,2,64]{1,3,2,0:T(8,128)(2,1)S(1)}, u32[]{:S(2)}) copy-start(bf16[6,256,2,64]{1,3,2,0:T(8,128)(2,1)S(1)} %get-tuple-element.504) | copy-start | bytes 1179652
  158.4 69.0 %copy-start.4 = (bf16[6,256,2,64]{1,3,2,0:T(8,128)(2,1)}, bf16[6,256,2,64]{1,3,2,0:T(8,128)(2,1)S(1)}, u32[]{:S(2)}) copy-start(bf16[6,256,2,64]{1,3,2,0:T(8,128)(2,1)S(1)} %get-tuple-element.157) | copy-start | bytes 1179652
  169.5 116.2 %copy-start.18 = (f32[256]{0:T(256)}, f32[256]{0:T(256)S(1)}, u32[]{:S(2)}) copy-start(f32[256]{0:T(256)S(1)} %fusion.153) | copy-start | bytes 3076
  169.6 106.5 %copy-start.6 = (bf16[1,256,768]{2,1,0:T(8,128)(2,1)S(1)}, bf16[1,256,768]{2,1,0:T(8,128)(2,1)}, u32[]{:S(2)}) copy-start(bf16[1,256,768]{2,1,0:T(8,128)(2,1)} %param.31) | copy-start | bytes 1179652
  276.0 7.5 copy-start.28
  283.5 2.2 copy-start.13
  286.1 3.9 copy-start.24
  287.7 2.2 copy-start.8
  378.5 77.3 %reduce-scatter.7.cloned.1.call-start = ((), (), s32[]{:S(2)}) async-start(), calls=%async_computation.6 | async-start | bytes 3932160 | tf_op jit(solution)/shard_map/reduce_scatter | solution.py:337
  379.3 157.8 %reduce-scatter.13.cloned.1.call-start = ((), (), s32[]{:S(2)}) async-start(), calls=%async_computation.9 | async-start | bytes 1253376 | tf_op jit(solution)/shard_map/reduce_scatter | solution.py:160
  381.1 214.9 %reduce-scatter.15.cloned.1.call-start = ((), (), s32[]{:S(2)}) async-start(), calls=%async_computation.10 | async-start | bytes 5013504 | tf_op jit(solution)/shard_map/reduce_scatter | solution.py:172
  385.9 289.1 %reduce-scatter.17.cloned.1.call-start = ((), (), s32[]{:S(2)}) async-start(), calls=%async_computation.11 | async-start | bytes 5013504 | tf_op jit(solution)/shard_map/reduce_scatter | solution.py:178
  393.4 63.6 %copy-start.12 = (bf16[6,256,2,64]{1,3,2,0:T(8,128)(2,1)S(1)}, bf16[6,256,2,64]{1,3,2,0:T(8,128)(2,1)}, u32[]{:S(2)}) copy-start(bf16[6,256,2,64]{1,3,2,0:T(8,128)(2,1)} %get-tuple-element.159) | copy-start | bytes 1179652
  393.4 63.6 %copy-start.17 = (f32[256]{0:T(256)S(1)}, f32[256]{0:T(256)}, u32[]{:S(2)}) copy-start(f32[256]{0:T(256)} %copy-done.16) | copy-start | bytes 3076
  393.4 63.6 %copy-start.20 = (f32[256]{0:T(256)S(1)}, f32[256]{0:T(256)}, u32[]{:S(2)}) copy-start(f32[256]{0:T(256)} %copy-done.19) | copy-start | bytes 3076
  393.4 63.6 %copy-start.27 = (f32[768]{0:T(1024)S(1)}, f32[768]{0:T(1024)}, u32[]{:S(2)}) copy-start(f32[768]{0:T(1024)} %copy-done.26) | copy-start | bytes 9220
  393.4 352.4 %reduce-scatter.11.cloned.1.call-start = ((), (), s32[]{:S(2)}) async-start(), calls=%async_computation.8 | async-start | bytes 3760128 | tf_op jit(solution)/shard_map/reduce_scatter | solution.py:154
  460.1 2.8 copy-start.30
  460.1 3.0 copy-start.10
  460.1 3.0 copy-start.11
  460.1 324.1 %all-reduce.22.cloned.1.call-start = ((), (), s32[]{:S(2)}) async-start(), calls=%async_computation.18 | async-start | bytes 1769472 | tf_op jit(solution)/shard_map/psum | solution.py:188
  466.9 279.0 %copy-start.2 = (f32[256,768]{1,0:T(8,128)S(1)}, f32[256,768]{1,0:T(8,128)}, u32[]{:S(2)}) copy-start(f32[256,768]{1,0:T(8,128)} %copy-done.1) | copy-start | bytes 2359300
  745.9 2.1 copy-start.31
  (13 other events, 16.7 us)
Sparse Core Ops, SparseCore 0:
  10.3 50.8 all-gather.20
  88.1 16.8 all-gather.24
  107.2 19.6 all-gather.22
  129.0 38.3 all-gather.26
  169.6 52.2 all-gather.28
  224.0 51.9 all-gather.30
  378.6 36.4 reduce-scatter.8
  417.8 37.9 reduce-scatter.6
  459.4 58.2 reduce-scatter.12
  521.4 74.5 reduce-scatter.14
  600.4 74.5 reduce-scatter.16
  678.7 67.1 reduce-scatter.10
  748.3 35.8 all-reduce.21
where the time goes:
time: 800 us; the launch traced here: 798 us
  waiting for transfers between devices  448 us (56%)
  matrix products  146 us (18%)
  blocking collectives  129 us (16%)
  other arithmetic  31.6 us (4%)
  local copies, waits for them, and re-layouts  23.4 us (3%)
  between operations  18.4 us (2%)
    unnamed x2, blocking collectives  124 us
    reduce_scatter x1, waiting for transfers between devices, settle(): lax.psum_scatter(partial_value[10].astype(jnp.bfloat16), ('fsdp', 'ctx'),...  79 us
    reduce_scatter x1, waiting for transfers between devices, settle(): lax.psum_scatter(partial_value[2].astype(jnp.bfloat16), ('fsdp', 'ctx'),...  70.9 us
    reduce_scatter x1, waiting for transfers between devices, settle(): lax.psum_scatter(partial_value[8].astype(jnp.bfloat16), ('fsdp', 'ctx'),...  58.9 us
    all_gather x1, waiting for transfers between devices, fetch_forward(): lax.all_gather(pieces[8], ('fsdp', 'ctx'), axis=0, tiled=True)  52.3 us
    all_gather x1, waiting for transfers between devices, fetch_forward(): lax.all_gather(pieces[10], ('fsdp', 'ctx'), axis=0, tiled=True)  48.6 us
    reduce_scatter x1, waiting for transfers between devices, layer_backward(): lax.psum_scatter(key_part, 'ctx', scatter_dimension=1, tiled=True)  39.5 us
    psum x1, waiting for transfers between devices, settle(): lax.psum(owned_parts[2].astype(jnp.bfloat16), 'rep').astype(jnp.float32)  31.2 us
  transfers between devices with their start and end apart: 13, of which 11 were waited for; matrix products, arithmetic and copies ran while one was open for 11% of the time, Pallas kernels for 0%

commit v1 on v0

v1 whole, which is shorter than its diff:
```python
import functools
import math

import jax
import jax.numpy as jnp
from jax import lax
from jax.experimental import pallas as pl
from jax.experimental.pallas import tpu as pltpu
from jax.sharding import PartitionSpec as P

H = 12
F32 = jnp.float32
BF16 = jnp.bfloat16
MASKED = -1e30
ROWS = 256


def dot(left, right, contract):
    return lax.dot_general(
        left, right, (((contract[0],), (contract[1],)), ((), ())), preferred_element_type=F32
    )


def norm_apply(values, gain_row, shift_row):
    center = values - jnp.mean(values, axis=-1, keepdims=True)
    spread = jnp.mean(center * center, axis=-1, keepdims=True)
    return center * lax.rsqrt(spread + 1e-05) * gain_row + shift_row


def norm_back(values, gain_row, upstream):
    center = values - jnp.mean(values, axis=-1, keepdims=True)
    scale = lax.rsqrt(jnp.mean(center * center, axis=-1, keepdims=True) + 1e-05)
    unit = center * scale
    e = upstream * gain_row
    grad = scale * (
        e - jnp.mean(e, axis=-1, keepdims=True) - unit * jnp.mean(e * unit, axis=-1, keepdims=True)
    )
    return grad, jnp.sum(upstream * unit, axis=0), jnp.sum(upstream, axis=0)


def causal(first_row, rows, keys):
    row = first_row + lax.broadcasted_iota(jnp.int32, (rows, keys), 0)
    key = lax.broadcasted_iota(jnp.int32, (rows, keys), 1)
    return key <= row


def attend_fwd(head, x, gain, shift, bias, w_joint, w_out, normed, joint, mix, logsum, part):
    length = x.shape[0]
    width = w_out.shape[0]
    heads = width // head
    factor = 1.0 / math.sqrt(head)
    for first in range(0, length, ROWS):
        rows = pl.ds(first, ROWS)
        last = first + ROWS
        h1 = norm_apply(x[rows, :].astype(F32), gain[...], shift[...]).astype(BF16)
        normed[rows, :] = h1
        joint[rows, :] = (dot(h1, w_joint[...], (1, 0)) + bias[...]).astype(BF16)
        allowed = causal(first, ROWS, last)
        outs = []
        for h in range(heads):
            q = joint[rows, pl.ds(h * head, head)]
            k = joint[pl.ds(0, last), pl.ds(width + h * head, head)]
            v = joint[pl.ds(0, last), pl.ds(2 * width + h * head, head)]
            s = jnp.where(allowed, dot(q, k, (1, 1)) * factor, MASKED)
            top = jnp.max(s, axis=-1, keepdims=True)
            p = jnp.exp(s - top)
            total = jnp.sum(p, axis=-1, keepdims=True)
            outs.append(dot((p * (1.0 / total)).astype(BF16), v, (1, 0)))
            logsum[rows, pl.ds(h, 1)] = top + jnp.log(total)
        o = jnp.concatenate(outs, axis=1).astype(BF16)
        mix[rows, :] = o
        part[rows, :] = dot(o, w_out[...], (1, 0)).astype(BF16)


def feed_both(h2, dm, w_up, b_up, w_down, part, dh2, d_up, d_down, d_bias, act, du):
    length = h2.shape[0]
    c0 = math.sqrt(2.0 / math.pi)
    d_bias[...] = jnp.zeros_like(d_bias)

    @pl.loop(0, length // ROWS)
    def _(at):
        rows = pl.ds(pl.multiple_of(at * ROWS, ROWS), ROWS)
        u = dot(h2[rows, :], w_up[...], (1, 0)) + b_up[...]
        square = u * u
        t = jnp.tanh(c0 * (u + 0.044715 * (u * square)))
        act[rows, :] = (0.5 * u * (1.0 + t)).astype(BF16)
        slope = 0.5 * (1.0 + t) + (0.5 * c0) * u * (1.0 - t * t) * (1.0 + (3 * 0.044715) * square)
        part[rows, :] = dot(act[rows, :], w_down[...], (1, 0)).astype(BF16)
        low = (dot(dm[rows, :], w_down[...], (1, 1)) * slope).astype(BF16)
        du[rows, :] = low
        d_bias[...] += jnp.sum(low.astype(F32), axis=0, keepdims=True)
        dh2[rows, :] = dot(low, w_up[...], (1, 1)).astype(BF16)

    d_up[...] = dot(h2[...], du[...], (0, 0)).astype(BF16)
    d_down[...] = dot(act[...], dm[...], (0, 0)).astype(BF16)


def attend_bwd(
    head, da, w_out, mix, joint, logsum, normed, w_joint, d_out, d_joint_w, sums, dh1, up, acc, low
):
    length = da.shape[0]
    width = w_out.shape[0]
    heads = width // head
    factor = 1.0 / math.sqrt(head)
    up[...] = dot(da[...], w_out[...], (1, 1)).astype(BF16)
    d_out[...] = dot(mix[...], da[...], (0, 0)).astype(BF16)
    for first in reversed(range(0, length, ROWS)):
        rows = pl.ds(first, ROWS)
        last = first + ROWS
        seen = pl.ds(0, last)
        allowed = causal(first, ROWS, last)
        for h in range(heads):
            qc = pl.ds(h * head, head)
            kc = pl.ds(width + h * head, head)
            vc = pl.ds(2 * width + h * head, head)
            q = joint[rows, qc]
            k = joint[seen, kc]
            v = joint[seen, vc]
            do = up[rows, qc]
            s = jnp.where(allowed, dot(q, k, (1, 1)) * factor, MASKED)
            p = jnp.exp(s - logsum[rows, pl.ds(h, 1)])
            dp = dot(do, v, (1, 1))
            center = jnp.sum(p * dp, axis=-1, keepdims=True)
            ds = (p * (dp - center)).astype(BF16)
            acc[rows, qc] = dot(ds, k, (1, 0)) * factor
            dk = dot(ds, q, (0, 0)) * factor
            dv = dot(p.astype(BF16), do, (0, 0))
            if last == length:
                acc[seen, kc] = dk
                acc[seen, vc] = dv
            else:
                acc[seen, kc] += dk
                acc[seen, vc] += dv
    low[...] = acc[...].astype(BF16)
    sums[...] = jnp.sum(low[...].astype(F32), axis=0, keepdims=True)
    d_joint_w[...] = dot(normed[...], low[...], (0, 0)).astype(BF16)
    for first in range(0, length, ROWS):
        rows = pl.ds(first, ROWS)
        dh1[rows, :] = dot(low[rows, :], w_joint[...], (1, 1)).astype(BF16)


def local_call(body, outs, scratch, flops, nbytes, args):
    return pl.pallas_call(
        body,
        out_shape=tuple(jax.ShapeDtypeStruct(shape, kind) for shape, kind in outs),
        in_specs=[pl.BlockSpec(memory_space=pltpu.VMEM)] * len(args),
        out_specs=tuple(pl.BlockSpec(memory_space=pltpu.VMEM) for _ in outs),
        scratch_shapes=[pltpu.VMEM(shape, kind) for shape, kind in scratch],
        compiler_params=pltpu.CompilerParams(vmem_limit_bytes=48 * 1024 * 1024),
        cost_estimate=pl.CostEstimate(flops=flops, bytes_accessed=nbytes, transcendentals=0),
    )(*args)


def swap_sum(value, replicas):
    low = value.astype(BF16)
    if replicas == 1:
        return low.astype(F32)
    if replicas == 2:
        other = lax.ppermute(low, "rep", [(0, 1), (1, 0)])
        return low.astype(F32) + other.astype(F32)
    return lax.psum(low, "rep").astype(F32)


def on_device(sizes, *args):
    replicas, nf, nc = sizes
    (
        tokens,
        g_one,
        s_one,
        w_joint,
        b_joint,
        w_attend,
        b_attend,
        g_two,
        s_two,
        w_expand,
        b_expand,
        w_contract,
        b_contract,
        cotangent,
    ) = args
    _, per_seq, d = tokens.shape
    length = per_seq * nc
    own = w_joint.shape[1]
    head = d // H
    width = d // nc
    part_ff = w_contract.shape[1]
    ff = part_ff * nf
    turn = [(f * nc + c, c * nc + f) for f in range(nf) for c in range(nc)]
    at_f, at_c = lax.axis_index("fsdp"), lax.axis_index("ctx")

    x_low = tokens[0]
    x_all = lax.all_gather(x_low, "ctx", axis=0, tiled=True)
    vec = jnp.concatenate(
        [v[0] for v in (g_one, s_one, b_attend, g_two, s_two, b_contract, b_joint, b_expand)]
    )
    count = vec.shape[0]
    pad = -own % 64
    block = w_joint[0].reshape(own, 3, nc, width).transpose(2, 0, 1, 3).reshape(nc, own, 3 * width)
    vec_rows = jnp.pad(vec.reshape(1, count), ((0, pad - 1), (0, 3 * width - count)))
    block = jnp.concatenate([block, jnp.broadcast_to(vec_rows[None], (nc, pad, 3 * width))], axis=1)
    block = lax.all_to_all(block, "ctx", 0, 0, tiled=True)
    block = lax.all_gather(block, "fsdp", axis=0, tiled=True)
    wj = block[:, :own].reshape(d, 3 * width)
    vecs = block[:, own, :count].astype(F32)
    g1, s1, ba, g2, s2, bc = (vecs[:, n * own : (n + 1) * own].reshape(1, d) for n in range(6))
    bj = vecs[:, 6 * own : 8 * own].reshape(2, nc, width)
    bj = lax.dynamic_index_in_dim(bj, at_c, 1, keepdims=False)
    bj = jnp.concatenate([bj[0], jnp.zeros((width,), F32), bj[1]]).reshape(1, 3 * width)
    be = vecs[:, 8 * own :].reshape(nf, nc, part_ff)
    be = lax.dynamic_index_in_dim(be, at_c, 1, keepdims=False).reshape(1, ff)

    wo = lax.ppermute(w_attend[0], ("fsdp", "ctx"), turn)
    wo = lax.all_gather(wo, "fsdp", axis=0, tiled=True)
    we = w_expand[0].reshape(own, nf, nc, part_ff).transpose(2, 0, 1, 3).reshape(nc, own, ff)
    we = lax.all_to_all(we, "ctx", 0, 0, tiled=True).reshape(nc * own, ff)
    we = lax.all_gather(we, "fsdp", axis=0, tiled=True)
    wc = lax.all_gather(w_contract[0], "fsdp", axis=0, tiled=True)
    dm_all = lax.all_gather(cotangent[0], "ctx", axis=0, tiled=True)

    normed, joint, mix, logsum, part = local_call(
        functools.partial(attend_fwd, head),
        (
            ((length, d), BF16),
            ((length, 3 * width), BF16),
            ((length, width), BF16),
            ((length, 128), F32),
            ((length, d), BF16),
        ),
        (),
        2 * length * d * 4 * width + 4 * length * length * width,
        12 * length * d,
        (x_all, g1, s1, bj, wj, wo),
    )
    x = x_low.astype(F32)
    mixed = lax.psum_scatter(part, "ctx", scatter_dimension=0, tiled=True).astype(F32)
    x1 = x + (mixed + ba)
    h2 = norm_apply(x1, g2, s2).astype(BF16)
    h2_all = lax.all_gather(h2, "ctx", axis=0, tiled=True)

    down, dh2, d_up, d_down, d_be = local_call(
        feed_both,
        (
            ((length, d), BF16),
            ((length, d), BF16),
            ((d, ff), BF16),
            ((ff, d), BF16),
            ((1, ff), F32),
        ),
        (((length, ff), BF16), ((length, ff), BF16)),
        12 * length * d * ff,
        18 * length * d,
        (h2_all, dm_all, we, be, wc),
    )
    dh2 = lax.psum_scatter(dh2, "ctx", scatter_dimension=0, tiled=True).astype(F32)
    dx = cotangent[0].astype(F32)
    back, d_g2, d_s2 = norm_back(x1, g2, dh2)
    dx1 = dx + back
    da = dx1.astype(BF16)
    da_all = lax.all_gather(da, "ctx", axis=0, tiled=True)
    down = lax.psum_scatter(down, "ctx", scatter_dimension=0, tiled=True).astype(F32)
    block_out = (x1 + (down + bc)).astype(BF16)

    d_wo, d_wj, sums, dh1 = local_call(
        functools.partial(attend_bwd, head),
        (
            ((width, d), BF16),
            ((d, 3 * width), BF16),
            ((1, 3 * width), F32),
            ((length, d), BF16),
        ),
        (
            ((length, width), BF16),
            ((length, 3 * width), F32),
            ((length, 3 * width), BF16),
        ),
        4 * length * d * 4 * width + 10 * length * length * width,
        12 * length * d,
        (da_all, wo, mix, joint, logsum, normed, wj),
    )
    dh1 = lax.psum_scatter(dh1, "ctx", scatter_dimension=0, tiled=True).astype(F32)
    back, d_g1, d_s1 = norm_back(x, g1, dh1)
    grad_tokens = dx1 + back

    out_wc = lax.psum_scatter(d_down, "fsdp", scatter_dimension=0, tiled=True)
    out_wc = swap_sum(out_wc, replicas)
    out_we = lax.psum_scatter(d_up, "fsdp", scatter_dimension=0, tiled=True)
    out_we = lax.all_to_all(out_we.reshape(nc, own, ff), "ctx", 0, 0, tiled=True)
    out_we = out_we.reshape(nc, own, nf, part_ff).transpose(1, 2, 0, 3).reshape(own, nf * nc * part_ff)
    out_we = swap_sum(out_we, replicas)
    out_wo = lax.psum_scatter(d_wo, "fsdp", scatter_dimension=0, tiled=True)
    out_wo = lax.ppermute(out_wo, ("fsdp", "ctx"), [(b, a) for a, b in turn])
    out_wo = swap_sum(out_wo, replicas)

    d_ba = jnp.sum(da.astype(F32), axis=0)
    d_bc = jnp.sum(dx, axis=0)
    mine = (jnp.arange(nc) == at_c).astype(F32)
    sums = sums.reshape(3, 1, width)
    d_bj = jnp.stack([sums[0], sums[2]]) * mine[None, :, None]
    d_be = d_be.reshape(nf, 1, part_ff) * mine[None, :, None]
    groups = nf * nc
    d_vec = jnp.concatenate(
        [v.reshape(groups, own) for v in (d_g1, d_s1, d_ba, d_g2, d_s2, d_bc)]
        + [d_bj.reshape(groups, 2 * own), d_be.reshape(groups, part_ff)],
        axis=1,
    ).astype(BF16)
    d_vec = jnp.pad(d_vec.reshape(groups, 1, count), ((0, 0), (0, pad - 1), (0, 3 * width - count)))
    tail = jnp.concatenate([d_wj.reshape(groups, own, 3 * width), d_vec], axis=1)
    tail = lax.psum_scatter(tail, "fsdp", scatter_dimension=0, tiled=True)
    tail = lax.all_to_all(tail, "ctx", 0, 0, tiled=True)
    out_vec = jnp.sum(tail[:, own, :count].astype(F32), axis=0)
    out_wj = tail[:, :own].reshape(nc, own, 3, width).transpose(1, 2, 0, 3).reshape(own, 3 * d)
    out_vec = swap_sum(out_vec.reshape(1, count), replicas)
    out_wj = swap_sum(out_wj, replicas)

    v = [out_vec[:, n * own : (n + 1) * own] for n in range(6)]
    return (
        block_out[None],
        grad_tokens[None],
        v[0],
        v[1],
        out_wj[None],
        out_vec[:, 6 * own : 8 * own],
        out_wo[None],
        v[2],
        v[3],
        v[4],
        out_we[None],
        out_vec[:, 8 * own :],
        out_wc[None],
        v[5],
    )


def solution(mesh):
    rows = P(("rep", "fsdp"), "ctx", None)
    vector = P(None, ("fsdp", "ctx"))
    matrix = P(None, ("fsdp", "ctx"), None)
    params = (
        vector,
        vector,
        matrix,
        vector,
        matrix,
        vector,
        vector,
        vector,
        matrix,
        vector,
        matrix,
        vector,
    )
    sizes = (mesh.shape["rep"], mesh.shape["fsdp"], mesh.shape["ctx"])
    return jax.shard_map(
        functools.partial(on_device, sizes),
        mesh=mesh,
        in_specs=(rows,) + params + (rows,),
        out_specs=(rows, rows) + params,
        check_vma=False,
    )
```

time: 800 us -> 518 us (0.65)
  matrix products: 146 us -> 0 us
  waiting for transfers between devices: 448 us -> 352 us
  blocking collectives: 129 us -> 56.1 us
  Pallas kernels: 0 us -> 39.6 us
  other arithmetic: 31.6 us -> 18.1 us
  starting transfers between devices: 0.92 us -> 13.3 us
    dot_general x54 -> x0, matrix products: 146 us -> none  [the longest x6 22.3 us: head_backward(): jnp.einsum('hqk,qhd->khd', score_grad, queries, preferred_element_type=jn...]
    unnamed x2 -> x0, blocking collectives: 124 us -> none
    reduce_scatter x6 -> x8, waiting for transfers between devices: 270 us -> 186 us  [the longest x1 30.7 us: on_device(): lax.psum_scatter(dh2, 'ctx', scatter_dimension=0, tiled=True).astype(F32)]
    pallas_call x0 -> x3, Pallas kernels: none -> 39.6 us  [local_call(): pl.pallas_call(body, out_shape=tuple((jax.ShapeDtypeStruct(shape, kind) f...]
    psum x1 -> x0, waiting for transfers between devices: 31.2 us -> none  [settle(): lax.psum(owned_parts[2].astype(jnp.bfloat16), 'rep').astype(jnp.float32)]
    all_to_all x0 -> x3, blocking collectives: none -> 30.1 us  [the longest x1 10.9 us: on_device(): block = lax.all_to_all(block, 'ctx', 0, 0, tiled=True)]
    all_gather x0 -> x1, blocking collectives: none -> 25.9 us  [on_device(): wo = lax.all_gather(wo, 'fsdp', axis=0, tiled=True)]
    another operation x17 -> x1, other arithmetic: 11.1 us -> 0.07 us  [the longest x12 11.1 us: on_device(): stacks = [jnp.stack([settled[0][member]]) for member in range(12)]]
  transfers between devices with their start and end apart: 13 -> 23, of which waited for: 11 -> 18; matrix products, arithmetic and copies ran while one was open for 11% -> 4% of each run, Pallas kernels for 0% -> 0%
where the time goes in v1:
time: 518 us; the launch traced here: 517 us
  waiting for transfers between devices  352 us (68%)
  blocking collectives  56.1 us (11%)
  Pallas kernels  39.6 us (8%)
  local copies, waits for them, and re-layouts  23.4 us (5%)
  other arithmetic  18.1 us (3%)
  between operations  14.4 us (3%)
  starting transfers between devices  13.3 us (3%)
    pallas_call x3, Pallas kernels, local_call(): pl.pallas_call(body, out_shape=tuple((jax.ShapeDtypeStruct(shape, kind) f...  39.6 us
    all_gather x1, waiting for transfers between devices, on_device(): we = lax.all_gather(we, 'fsdp', axis=0, tiled=True)  31.1 us
    reduce_scatter x1, waiting for transfers between devices, on_device(): lax.psum_scatter(dh2, 'ctx', scatter_dimension=0, tiled=True).astype(F32)  30.7 us
    reduce_scatter x1, waiting for transfers between devices, on_device(): out_we = lax.psum_scatter(d_up, 'fsdp', scatter_dimension=0, tiled=True)  28.8 us
    all_gather x1, waiting for transfers between devices, on_device(): wc = lax.all_gather(w_contract[0], 'fsdp', axis=0, tiled=True)  28 us
    reduce_scatter x1, waiting for transfers between devices, on_device(): lax.psum_scatter(down, 'ctx', scatter_dimension=0, tiled=True).astype(F32)  27.3 us
    reduce_scatter x1, waiting for transfers between devices, on_device(): out_wc = lax.psum_scatter(d_down, 'fsdp', scatter_dimension=0, tiled=True)  27.2 us
    all_gather x1, blocking collectives, on_device(): wo = lax.all_gather(wo, 'fsdp', axis=0, tiled=True)  25.9 us
  transfers between devices with their start and end apart: 23, of which 18 were waited for; matrix products, arithmetic and copies ran while one was open for 4% of the time, Pallas kernels for 0%

profile of v1, /device:TPU:0, one launch (start us, length us, event | category | flops | bytes accessed | tf_op | source)
XLA Modules:
  0.0 517.0 jit_solution(10920907559823292011)
XLA Ops:
  7.9 4.8 concatenate.39
  14.5 10.9 %all_to_all.20 = bf16[4,64,576]{2,1,0:T(8,128)(2,1)} all-to-all(bf16[4,64,576]{2,1,0:T(8,128)(2,1)S(1)} %pad_maximum_fusion), channel_id=1, replica_groups=mesh['rep'=2,'fsdp'=4,'ctx'=4] {'ctx'}, dimensions={0} | all-to-all | bytes 589824 | tf_op jit(solution)/shard_map/all_to_all | solution.py:202
  26.9 25.9 %all_gather.26.w_out = bf16[192,768]{1,0:T(8,128)(2,1)S(1)} all-gather(bf16[48,768]{1,0:T(8,128)(2,1)S(1)} %collective-permute-done), channel_id=1, replica_groups=mesh['rep'=2,'fsdp'=4,'ctx'=4] {'fsdp'}, dimensions={0}, use_global_device_ids=true | all-gather | bytes 368640 | tf_op jit(solution)/shard_map/all_gather | solution.py:214
  52.8 10.9 %all-gather.11.cloned.1.call-done = bf16[16,64,576]{2,1,0:T(8,128)(2,1)} async-done(((bf16[4,64,576]{2,1,0:T(8,128)(2,1)}), bf16[16,64,576]{2,1,0:T(8,128)(2,1)}) %all-gather.11.cloned.1.call-update) | async-done | bytes 1179664 | tf_op jit(solution)/shard_map/all_gather | solution.py:203
  67.0 16.9 %all-gather.19.cloned.1.call-done = bf16[1,1024,768]{2,1,0:T(8,128)(2,1)} async-done(((bf16[1,256,768]{2,1,0:T(8,128)(2,1)}), bf16[1,1024,768]{2,1,0:T(8,128)(2,1)}) %all-gather.19.cloned.1.call-update) | async-done | bytes 1572880 | tf_op jit(solution)/shard_map/all_gather | solution.py:193
  83.9 11.1 %shard_map.245 = (bf16[1024,768]{1,0:T(8,128)(2,1)S(1)}, bf16[1024,576]{1,0:T(8,128)(2,1)S(1)}, bf16[1024,192]{1,0:T(8,128)(2,1)S(1)}, f32[1024,128]{1,0:T(8,128)S(1)}, bf16[1024,768]{1,0:T(8,128)(2,1)}) custom-call(bf16[1024,768]{1,0:T(8,128)(2,1)} %bitcast.119, f32[1,768]{1,0:T(1,128)S(1)} %reshape.327.gain, f32[1,768]{1,0:T(1,128)S(1)} %reshape.328.shift, ...), custom_call_target="tpu_custom_call" | custom-call | flops 2013265920 | bytes 9437184 | tf_op jit(solution)/shard_map/pallas_call | solution.py:143
  99.3 9.5 %all_to_all.21 = bf16[4,48,768]{2,1,0:T(8,128)(2,1)} all-to-all(bf16[4,48,768]{2,1,0:T(8,128)(2,1)S(1)} %reshape.332), channel_id=1, replica_groups=mesh['rep'=2,'fsdp'=4,'ctx'=4] {'ctx'}, dimensions={0} | all-to-all | bytes 589824 | tf_op jit(solution)/shard_map/all_to_all | solution.py:216
  111.7 14.0 %reduce-scatter.9.cloned.1.call-done = bf16[256,768]{1,0:T(8,128)(2,1)} async-done(((bf16[1024,768]{1,0:T(8,128)(2,1)}), bf16[256,768]{1,0:T(8,128)(2,1)}) %reduce-scatter.9.cloned.1.call-update) | async-done | bytes 393232 | tf_op jit(solution)/shard_map/reduce_scatter | solution.py:236
  129.7 28.0 %all-gather.23.cloned.1.call-done = bf16[1,768,768]{2,1,0:T(8,128)(2,1)} async-done(((bf16[1,192,768]{2,1,0:T(8,128)(2,1)}), bf16[1,768,768]{2,1,0:T(8,128)(2,1)}) %all-gather.23.cloned.1.call-update) | async-done | bytes 1179664 | tf_op jit(solution)/shard_map/all_gather | solution.py:218
  157.6 31.1 %all-gather.15.cloned.1.call-done.w_up = bf16[768,768]{1,0:T(8,128)(2,1)} async-done(((bf16[192,768]{1,0:T(8,128)(2,1)}), bf16[768,768]{1,0:T(8,128)(2,1)}) %all-gather.15.cloned.1.call-update) | async-done | bytes 1179664 | tf_op jit(solution)/shard_map/all_gather | solution.py:217
  188.7 20.3 %all-gather.21.cloned.1.call-done = bf16[1,1024,768]{2,1,0:T(8,128)(2,1)} async-done(((bf16[1,256,768]{2,1,0:T(8,128)(2,1)}), bf16[1,1024,768]{2,1,0:T(8,128)(2,1)}) %all-gather.21.cloned.1.call-update) | async-done | bytes 1572880 | tf_op jit(solution)/shard_map/all_gather | solution.py:219
  209.0 21.9 %all-gather.13.cloned.1.call-done.h2 = bf16[1024,768]{1,0:T(8,128)(2,1)} async-done(((bf16[256,768]{1,0:T(8,128)(2,1)}), bf16[1024,768]{1,0:T(8,128)(2,1)}) %all-gather.13.cloned.1.call-update) | async-done | bytes 1572880 | tf_op jit(solution)/shard_map/all_gather | solution.py:239
  233.5 12.2 %shard_map.246 = (bf16[1024,768]{1,0:T(8,128)(2,1)}, bf16[1024,768]{1,0:T(8,128)(2,1)}, bf16[768,768]{1,0:T(8,128)(2,1)}, bf16[768,768]{1,0:T(8,128)(2,1)}, f32[1,768]{1,0:T(1,128)S(1)}) custom-call(bf16[1024,768]{1,0:T(8,128)(2,1)} %all-gather.13.cloned.1.call-done.h2, bf16[1024,768]{1,0:T(8,128)(2,1)} %bitcast.120, bf16[768,768]{1,0:T(8,128)(2,1)S(1)} %copy-done.1, ...), custom_call_target="tpu_custom_call" | custom-call | flops 7247757312 | bytes 14155776 | tf_op jit(solution)/shard_map/pallas_call | solution.py:143
  246.8 27.3 %reduce-scatter.11.cloned.1.call-done = bf16[256,768]{1,0:T(8,128)(2,1)} async-done(((bf16[1024,768]{1,0:T(8,128)(2,1)}), bf16[256,768]{1,0:T(8,128)(2,1)}) %reduce-scatter.11.cloned.1.call-update) | async-done | bytes 393232 | tf_op jit(solution)/shard_map/reduce_scatter | solution.py:261
  274.1 30.7 %reduce-scatter.13.cloned.1.call-done = bf16[256,768]{1,0:T(8,128)(2,1)} async-done(((bf16[1024,768]{1,0:T(8,128)(2,1)}), bf16[256,768]{1,0:T(8,128)(2,1)}) %reduce-scatter.13.cloned.1.call-update) | async-done | bytes 393232 | tf_op jit(solution)/shard_map/reduce_scatter | solution.py:255
  304.8 2.6 fusion.22
  309.0 19.8 %all-gather.17.cloned.1.call-done.da = bf16[1024,768]{1,0:T(8,128)(2,1)} async-done(((bf16[256,768]{1,0:T(8,128)(2,1)}), bf16[1024,768]{1,0:T(8,128)(2,1)}) %all-gather.17.cloned.1.call-update) | async-done | bytes 1572880 | tf_op jit(solution)/shard_map/all_gather | solution.py:260
  330.1 16.3 %shard_map.247 = (bf16[192,768]{1,0:T(8,128)(2,1)}, bf16[768,576]{1,0:T(8,128)(2,1)S(1)}, f32[1,576]{1,0:T(1,128)S(1)}, bf16[1024,768]{1,0:T(8,128)(2,1)}) custom-call(bf16[1024,768]{1,0:T(8,128)(2,1)} %all-gather.17.cloned.1.call-done.da, bf16[192,768]{1,0:T(8,128)(2,1)S(1)} %all_gather.26.w_out, bf16[1024,192]{1,0:T(8,128)(2,1)S(1)} %get-tuple-element.31.mix, ...), custom_call_target="tpu_custom_call" | custom-call | flops 4429185024 | bytes 9437184 | tf_op jit(solution)/shard_map/pallas_call | solution.py:143
  349.1 25.6 %reduce-scatter.15.cloned.1.call-done = bf16[256,768]{1,0:T(8,128)(2,1)} async-done(((bf16[1024,768]{1,0:T(8,128)(2,1)}), bf16[256,768]{1,0:T(8,128)(2,1)}) %reduce-scatter.15.cloned.1.call-update) | async-done | bytes 393232 | tf_op jit(solution)/shard_map/reduce_scatter | solution.py:281
  378.8 27.2 %reduce-scatter.23.cloned.1.call-done = bf16[192,768]{1,0:T(8,128)(2,1)} async-done(((bf16[768,768]{1,0:T(8,128)(2,1)}), bf16[192,768]{1,0:T(8,128)(2,1)}) %reduce-scatter.23.cloned.1.call-update) | async-done | bytes 294928 | tf_op jit(solution)/shard_map/reduce_scatter | solution.py:285
  407.5 28.8 %reduce-scatter.21.cloned.1.call-done = bf16[192,768]{1,0:T(8,128)(2,1)} async-done(((bf16[768,768]{1,0:T(8,128)(2,1)}), bf16[192,768]{1,0:T(8,128)(2,1)}) %reduce-scatter.21.cloned.1.call-update) | async-done | bytes 294928 | tf_op jit(solution)/shard_map/reduce_scatter | solution.py:287
  436.3 9.8 %all_to_all.22 = bf16[4,48,768]{2,1,0:T(8,128)(2,1)S(1)} all-to-all(bf16[4,48,768]{2,1,0:T(8,128)(2,1)} %bitcast.109), channel_id=1, replica_groups=mesh['rep'=2,'fsdp'=4,'ctx'=4] {'ctx'}, dimensions={0} | all-to-all | bytes 589824 | tf_op jit(solution)/shard_map/all_to_all | solution.py:288
  447.3 1.5 collective-permute-start.5
  448.8 8.8 %reduce-scatter.19.cloned.1.call-done = bf16[48,768]{1,0:T(8,128)(2,1)} async-done(((bf16[192,768]{1,0:T(8,128)(2,1)}), bf16[48,768]{1,0:T(8,128)(2,1)}) %reduce-scatter.19.cloned.1.call-update) | async-done | bytes 73744 | tf_op jit(solution)/shard_map/reduce_scatter | solution.py:291
  457.6 1.5 collective-permute-start.3
  460.0 1.5 collective-permute-start.4
  462.4 2.2 collective-permute-done.4
  465.2 24.0 %reduce-scatter.17.cloned.1.call-done = bf16[4,64,576]{2,1,0:T(8,128)(2,1)} async-done(((bf16[16,64,576]{2,1,0:T(8,128)(2,1)}), bf16[4,64,576]{2,1,0:T(8,128)(2,1)}) %reduce-scatter.17.cloned.1.call-update) | async-done | bytes 294928 | tf_op jit(solution)/shard_map/reduce_scatter | solution.py:309
  489.2 3.5 all-to-all-start.2
  492.7 6.7 %all-to-all-done.2 = bf16[4,64,576]{2,1,0:T(8,128)(2,1)S(1)} async-done(((bf16[4,64,576]{2,1,0:T(8,128)(2,1)}), bf16[4,64,576]{2,1,0:T(8,128)(2,1)S(1)}, u32[]{:S(2)}, u32[]{:S(2)}) %all-to-all-start.2) | async-done | bytes 294944 | tf_op jit(solution)/shard_map/all_to_all | solution.py:310
  499.4 1.5 collective-permute-start.1
  505.3 4.4 collective-permute-done.2
  (174 shorter events, 41.7 us)
Async XLA Ops:
  7.2 56.5 %all-gather.11.cloned.1.call-start = ((), (), s32[]{:S(2)}) async-start(), calls=%async_computation.12 | async-start | bytes 1638400 | tf_op jit(solution)/shard_map/all_gather | solution.py:203
  25.4 58.5 %all-gather.19.cloned.1.call-start = ((), (), s32[]{:S(2)}) async-start(), calls=%async_computation.24 | async-start | bytes 1966080 | tf_op jit(solution)/shard_map/all_gather | solution.py:193
  26.1 99.5 %reduce-scatter.9.cloned.1.call-start = ((), (), s32[]{:S(2)}) async-start(), calls=%async_computation.13 | async-start | bytes 1966080 | tf_op jit(solution)/shard_map/reduce_scatter | solution.py:236
  26.2 0.7 collective-permute-start
  65.6 29.4 %copy-start.15 = (f32[16,48]{1,0:T(8,128)}, f32[16,48]{1,0:T(8,128)S(1)}, u32[]{:S(2)}) copy-start(f32[16,48]{1,0:T(8,128)S(1)} %get-tuple-element.59) | copy-start | bytes 9220
  97.3 60.3 %all-gather.23.cloned.1.call-start = ((), (), s32[]{:S(2)}) async-start(), calls=%async_computation.26 | async-start | bytes 1474560 | tf_op jit(solution)/shard_map/all_gather | solution.py:218
  97.9 90.8 %all-gather.15.cloned.1.call-start = ((), (), s32[]{:S(2)}) async-start(), calls=%async_computation.15 | async-start | bytes 1474560 | tf_op jit(solution)/shard_map/all_gather | solution.py:217
  108.7 100.3 %all-gather.21.cloned.1.call-start = ((), (), s32[]{:S(2)}) async-start(), calls=%async_computation.25 | async-start | bytes 1966080 | tf_op jit(solution)/shard_map/all_gather | solution.py:219
  109.3 121.6 %all-gather.13.cloned.1.call-start = ((), (), s32[]{:S(2)}) async-start(), calls=%async_computation.14 | async-start | bytes 1966080 | tf_op jit(solution)/shard_map/all_gather | solution.py:239
  129.3 144.8 %reduce-scatter.11.cloned.1.call-start = ((), (), s32[]{:S(2)}) async-start(), calls=%async_computation.16 | async-start | bytes 1966080 | tf_op jit(solution)/shard_map/reduce_scatter | solution.py:261
  245.7 59.1 %copy-start.18 = (f32[768]{0:T(1024)S(1)}, f32[768]{0:T(1024)}, u32[]{:S(2)}) copy-start(f32[768]{0:T(1024)} %copy-done.17) | copy-start | bytes 9220
  245.7 59.1 %copy-start.21 = (f32[256]{0:T(256)S(1)}, f32[256]{0:T(256)}, u32[]{:S(2)}) copy-start(f32[256]{0:T(256)} %copy-done.20) | copy-start | bytes 3076
  245.7 59.1 %copy-start.23 = (f32[256]{0:T(256)S(1)}, f32[256]{0:T(256)}, u32[]{:S(2)}) copy-start(f32[256]{0:T(256)} %copy-done.22) | copy-start | bytes 3076
  245.8 59.1 %reduce-scatter.13.cloned.1.call-start = ((), (), s32[]{:S(2)}) async-start(), calls=%async_computation.17 | async-start | bytes 1966080 | tf_op jit(solution)/shard_map/reduce_scatter | solution.py:255
  246.5 61.0 %copy-start.9 = (bf16[1,256,768]{2,1,0:T(8,128)(2,1)S(1)}, bf16[1,256,768]{2,1,0:T(8,128)(2,1)}, u32[]{:S(2)}) copy-start(bf16[1,256,768]{2,1,0:T(8,128)(2,1)} %param.27) | copy-start | bytes 1179652
  246.5 82.2 %all-gather.17.cloned.1.call-start = ((), (), s32[]{:S(2)}) async-start(), calls=%async_computation.18 | async-start | bytes 1966080 | tf_op jit(solution)/shard_map/all_gather | solution.py:260
  308.9 65.7 %reduce-scatter.15.cloned.1.call-start = ((), (), s32[]{:S(2)}) async-start(), calls=%async_computation.19 | async-start | bytes 1966080 | tf_op jit(solution)/shard_map/reduce_scatter | solution.py:281
  346.4 59.7 %reduce-scatter.23.cloned.1.call-start = ((), (), s32[]{:S(2)}) async-start(), calls=%async_computation.23 | async-start | bytes 1474560 | tf_op jit(solution)/shard_map/reduce_scatter | solution.py:285
  346.4 29.4 %copy-start.6 = (bf16[1,256,768]{2,1,0:T(8,128)(2,1)S(1)}, bf16[1,256,768]{2,1,0:T(8,128)(2,1)}, u32[]{:S(2)}) copy-start(bf16[1,256,768]{2,1,0:T(8,128)(2,1)} %param.14) | copy-start | bytes 1179652
  347.0 89.3 %reduce-scatter.21.cloned.1.call-start = ((), (), s32[]{:S(2)}) async-start(), calls=%async_computation.22 | async-start | bytes 1474560 | tf_op jit(solution)/shard_map/reduce_scatter | solution.py:287
  347.7 109.9 %reduce-scatter.19.cloned.1.call-start = ((), (), s32[]{:S(2)}) async-start(), calls=%async_computation.21 | async-start | bytes 368640 | tf_op jit(solution)/shard_map/reduce_scatter | solution.py:291
  348.9 140.4 %reduce-scatter.17.cloned.1.call-start = ((), (), s32[]{:S(2)}) async-start(), calls=%async_computation.20 | async-start | bytes 1638400 | tf_op jit(solution)/shard_map/reduce_scatter | solution.py:309
  406.1 53.1 %copy-start.14 = (bf16[192,768]{1,0:T(8,128)(2,1)S(1)}, bf16[192,768]{1,0:T(8,128)(2,1)}, u32[]{:S(2)}) copy-start(bf16[192,768]{1,0:T(8,128)(2,1)} %reduce-scatter.23.cloned.1.call-done) | copy-start | bytes 884740
  406.1 53.1 %collective-permute-start.6 = (bf16[192,768]{1,0:T(8,128)(2,1)}, bf16[192,768]{1,0:T(8,128)(2,1)S(1)}, u32[]{:S(2)}, u32[]{:S(2)}) collective-permute-start(bf16[192,768]{1,0:T(8,128)(2,1)} %reduce-scatter.23.cloned.1.call-done), channel_id=1, source_target_pairs={{0,16},{16,0},{1,17},{17,1},{2,18},{18,2},{3,19},{19,3},{4,20},{20... | collective-permute-start | bytes 884744 | tf_op jit(solution)/shard_map/ppermute | solution.py:159
  447.2 53.7 %copy-start.8 = (bf16[256,768]{1,0:T(8,128)(2,1)S(1)}, bf16[256,768]{1,0:T(8,128)(2,1)}, u32[]{:S(2)}) copy-start(bf16[256,768]{1,0:T(8,128)(2,1)} %reduce-scatter.15.cloned.1.call-done) | copy-start | bytes 1179652
  447.3 53.7 %copy-start.11 = (f32[256,768]{1,0:T(8,128)S(1)}, f32[256,768]{1,0:T(8,128)}, u32[]{:S(2)}) copy-start(f32[256,768]{1,0:T(8,128)} %get-tuple-element.51) | copy-start | bytes 2359300
  447.3 14.2 %collective-permute-start.5 = (bf16[48,3072]{1,0:T(8,128)(2,1)S(1)}, bf16[48,3072]{1,0:T(8,128)(2,1)S(1)}, u32[]{:S(2)}, u32[]{:S(2)}) collective-permute-start(bf16[48,3072]{1,0:T(8,128)(2,1)S(1)} %reshape.341), channel_id=1, source_target_pairs={{0,16},{16,0},{1,17},{17,1},{2,18},{18,2},{3,19},{19,3},{4,20},{20... | collective-permute-start | bytes 884744 | tf_op jit(solution)/shard_map/ppermute | solution.py:159
  457.6 2.4 collective-permute-start.3
  460.0 4.5 collective-permute-start.4
  489.2 10.2 %all-to-all-start.2 = ((bf16[4,64,576]{2,1,0:T(8,128)(2,1)}), bf16[4,64,576]{2,1,0:T(8,128)(2,1)S(1)}, u32[]{:S(2)}, u32[]{:S(2)}) async-start(bf16[4,64,576]{2,1,0:T(8,128)(2,1)} %reduce-scatter.17.cloned.1.call-done), calls=%async_computation.7 | async-start | bytes 655360 | tf_op jit(solution)/shard_map/all_to_all | solution.py:310
  499.4 4.1 collective-permute-start.1
  502.9 6.8 %collective-permute-start.2 = (bf16[48,2304]{1,0:T(8,128)(2,1)S(1)}, bf16[48,2304]{1,0:T(8,128)(2,1)S(1)}, u32[]{:S(2)}, u32[]{:S(2)}) collective-permute-start(bf16[48,2304]{1,0:T(8,128)(2,1)S(1)} %reshape.338), channel_id=1, source_target_pairs={{0,16},{16,0},{1,17},{17,1},{2,18},{18,2},{3,19},{19,3},{4,20},{20... | collective-permute-start | bytes 663560 | tf_op jit(solution)/shard_map/ppermute | solution.py:159
  (16 other events, 77.6 us)
Sparse Core Ops, SparseCore 0:
  25.5 38.1 all-gather.10
  65.2 18.6 all-gather.18
  97.4 28.1 reduce-scatter.8
  127.2 30.4 all-gather.22
  159.1 29.5 all-gather.14
  190.2 18.7 all-gather.20
  211.2 19.6 all-gather.12
  245.9 28.1 reduce-scatter.10
  276.6 28.1 reduce-scatter.12
  309.1 19.6 all-gather.16
  346.5 28.1 reduce-scatter.14
  376.8 29.1 reduce-scatter.22
  408.4 27.8 reduce-scatter.20
  439.0 18.5 reduce-scatter.18
  459.8 29.4 reduce-scatter.16

commit v2 on v1

--- a/solution.py
+++ b/solution.py
@@ -151,6 +151,228 @@
     )(*args)
 
 
+CHUNKS = 4
+
+
+class Ctx:
+    def __init__(self, send_sem, recv_sem):
+        self.me = lax.axis_index("ctx")
+        high, low = self.me // 2, self.me % 2
+        self.sibling = high * 2 + (1 - low)
+        self.across = (1 - high) * 2 + low
+        self.diagonal = (1 - high) * 2 + (1 - low)
+        self.send_sem, self.recv_sem = send_sem, recv_sem
+        self.sent = []
+
+    def enter(self):
+        barrier = pltpu.get_barrier_semaphore()
+        for partner in (self.sibling, self.across):
+            pl.semaphore_signal(
+                barrier,
+                inc=1,
+                device_id={"ctx": partner},
+                device_id_type=pl.DeviceIdType.MESH,
+            )
+        pl.semaphore_wait(barrier, 2)
+
+    def send(self, src, dst, slot, partner):
+        copy = pltpu.make_async_remote_copy(
+            src_ref=src,
+            dst_ref=dst,
+            send_sem=self.send_sem.at[slot],
+            recv_sem=self.recv_sem.at[slot],
+            device_id={"ctx": partner},
+            device_id_type=pl.DeviceIdType.MESH,
+        )
+        copy.start()
+        self.sent.append(copy)
+        return copy
+
+    def leave(self):
+        for copy in self.sent:
+            copy.wait_send()
+
+
+def block_rows(block, rows, chunk):
+    size = rows // CHUNKS
+    return pl.ds(pl.multiple_of(block * rows + chunk * size, size), size)
+
+
+def gather_send(ctx, whole, rows, chunk, slot):
+    at = block_rows(ctx.me, rows, chunk)
+    return (
+        ctx.send(whole.at[at], whole.at[at], slot + 1, ctx.across),
+        ctx.send(whole.at[at], whole.at[at], slot, ctx.sibling),
+    )
+
+
+def gather_finish(ctx, whole, rows, copies, slot):
+    passed = []
+    for chunk in range(CHUNKS):
+        copies[chunk][0].wait_recv()
+        at = block_rows(ctx.across, rows, chunk)
+        passed.append(ctx.send(whole.at[at], whole.at[at], slot + 3 * chunk + 2, ctx.sibling))
+    for chunk in range(CHUNKS):
+        copies[chunk][1].wait_recv()
+        passed[chunk].wait_recv()
+
+
+def scatter_start(ctx, part, near, rows, slot):
+    copies = []
+    size = rows // CHUNKS
+    for side, block in enumerate((ctx.diagonal, ctx.sibling)):
+        for chunk in range(CHUNKS):
+            copies.append(
+                ctx.send(
+                    part.at[block_rows(block, rows, chunk)],
+                    near.at[side, pl.ds(chunk * size, size)],
+                    slot + side * CHUNKS + chunk,
+                    ctx.sibling,
+                )
+            )
+    return copies
+
+
+def scatter_across(ctx, part, near, out, far, rows, copies, slot):
+    size = rows // CHUNKS
+    for chunk in range(CHUNKS):
+        copies[chunk].wait_recv()
+        here = pl.ds(chunk * size, size)
+        out[here, :] = (
+            part[block_rows(ctx.across, rows, chunk), :].astype(F32) + near[0, here, :].astype(F32)
+        ).astype(BF16)
+        copies.append(
+            ctx.send(out.at[here], far.at[here], slot + 2 * CHUNKS + chunk, ctx.across)
+        )
+
+
+def scatter_take(ctx, part, near, far, rows, copies, chunk):
+    size = rows // CHUNKS
+    here = pl.ds(chunk * size, size)
+    copies[CHUNKS + chunk].wait_recv()
+    copies[2 * CHUNKS + chunk].wait_recv()
+    own = part[block_rows(ctx.me, rows, chunk), :].astype(F32)
+    return own + near[1, here, :].astype(F32) + far[here, :].astype(F32)
+
+
+def gather_inputs(x, up, x_all, up_all, send_sem, recv_sem):
+    ctx = Ctx(send_sem, recv_sem)
+    ctx.enter()
+    rows = x.shape[0]
+    size = rows // CHUNKS
+    kept = []
+    for index, (own, whole) in enumerate(((x, x_all), (up, up_all))):
+        copies = []
+        for chunk in range(CHUNKS):
+            whole[block_rows(ctx.me, rows, chunk), :] = own[pl.ds(chunk * size, size), :]
+            copies.append(gather_send(ctx, whole, rows, chunk, 3 * CHUNKS * index + 3 * chunk))
+        kept.append(copies)
+    for index, whole in enumerate((x_all, up_all)):
+        gather_finish(ctx, whole, rows, kept[index], 3 * CHUNKS * index)
+    ctx.leave()
+
+
+def between_forward(
+    part, x, bias, gain, shift, x1, whole, near, out, far, send_sem, recv_sem
+):
+    ctx = Ctx(send_sem, recv_sem)
+    ctx.enter()
+    rows = x.shape[0]
+    size = rows // CHUNKS
+    arrived = scatter_start(ctx, part, near, rows, 0)
+    scatter_across(ctx, part, near, out, far, rows, arrived, 0)
+    copies = []
+    for chunk in range(CHUNKS):
+        here = pl.ds(chunk * size, size)
+        total = scatter_take(ctx, part, near, far, rows, arrived, chunk)
+        value = x[here, :].astype(F32) + (total + bias[...])
+        x1[here, :] = value
+        whole[block_rows(ctx.me, rows, chunk), :] = norm_apply(
+            value, gain[...], shift[...]
+        ).astype(BF16)
+        copies.append(gather_send(ctx, whole, rows, chunk, 3 * CHUNKS + 3 * chunk))
+    gather_finish(ctx, whole, rows, copies, 3 * CHUNKS)
+    ctx.leave()
+
+
+def between_backward(
+    part, x1, up, gain, dx1, whole, d_gain, d_shift, d_bias, near, out, far, send_sem, recv_sem
+):
+    ctx = Ctx(send_sem, recv_sem)
+    ctx.enter()
+    rows = x1.shape[0]
+    size = rows // CHUNKS
+    arrived = scatter_start(ctx, part, near, rows, 0)
+    for total in (d_gain, d_shift, d_bias):
+        total[...] = jnp.zeros_like(total)
+    scatter_across(ctx, part, near, out, far, rows, arrived, 0)
+    copies = []
+    for chunk in range(CHUNKS):
+        here = pl.ds(chunk * size, size)
+        total = scatter_take(ctx, part, near, far, rows, arrived, chunk)
+        back, gain_part, shift_part = norm_back(x1[here, :], gain[...], total)
+        value = up[here, :].astype(F32) + back
+        dx1[here, :] = value
+        low = value.astype(BF16)
+        whole[block_rows(ctx.me, rows, chunk), :] = low
+        copies.append(gather_send(ctx, whole, rows, chunk, 3 * CHUNKS + 3 * chunk))
+        d_gain[...] += gain_part[None]
+        d_shift[...] += shift_part[None]
+        d_bias[...] += jnp.sum(low.astype(F32), axis=0, keepdims=True)
+    gather_finish(ctx, whole, rows, copies, 3 * CHUNKS)
+    ctx.leave()
+
+
+def sum_block(down, x1, bias, block, near, out, far, send_sem, recv_sem):
+    ctx = Ctx(send_sem, recv_sem)
+    ctx.enter()
+    rows = x1.shape[0]
+    size = rows // CHUNKS
+    arrived = scatter_start(ctx, down, near, rows, 0)
+    scatter_across(ctx, down, near, out, far, rows, arrived, 0)
+    for chunk in range(CHUNKS):
+        here = pl.ds(chunk * size, size)
+        total = scatter_take(ctx, down, near, far, rows, arrived, chunk)
+        block[here, :] = (x1[here, :] + (total + bias[...])).astype(BF16)
+    ctx.leave()
+
+
+def sum_grad(grad, x, gain, dx1, dx, d_gain, d_shift, near, out, far, send_sem, recv_sem):
+    ctx = Ctx(send_sem, recv_sem)
+    ctx.enter()
+    rows = x.shape[0]
+    size = rows // CHUNKS
+    arrived = scatter_start(ctx, grad, near, rows, 0)
+    for total in (d_gain, d_shift):
+        total[...] = jnp.zeros_like(total)
+    scatter_across(ctx, grad, near, out, far, rows, arrived, 0)
+    for chunk in range(CHUNKS):
+        here = pl.ds(chunk * size, size)
+        total = scatter_take(ctx, grad, near, far, rows, arrived, chunk)
+        back, gain_part, shift_part = norm_back(x[here, :].astype(F32), gain[...], total)
+        dx[here, :] = dx1[here, :] + back
+        d_gain[...] += gain_part[None]
+        d_shift[...] += shift_part[None]
+    ctx.leave()
+
+
+def linked_call(body, number, outs, scratch, slots, args):
+    return pl.pallas_call(
+        body,
+        out_shape=tuple(jax.ShapeDtypeStruct(shape, kind) for shape, kind in outs),
+        in_specs=[pl.BlockSpec(memory_space=pltpu.VMEM)] * len(args),
+        out_specs=tuple(pl.BlockSpec(memory_space=pltpu.VMEM) for _ in outs),
+        scratch_shapes=[pltpu.VMEM(shape, kind) for shape, kind in scratch]
+        + [pltpu.SemaphoreType.DMA((slots,)), pltpu.SemaphoreType.DMA((slots,))],
+        compiler_params=pltpu.CompilerParams(
+            collective_id=number, has_side_effects=True, vmem_limit_bytes=32 * 1024 * 1024
+        ),
+        cost_estimate=pl.CostEstimate(
+            flops=10_000_000_000, bytes_accessed=40_000_000, transcendentals=0
+        ),
+    )(*args)
+
+
 def swap_sum(value, replicas):
     low = value.astype(BF16)
     if replicas == 1:
@@ -190,7 +412,11 @@
     at_f, at_c = lax.axis_index("fsdp"), lax.axis_index("ctx")
 
     x_low = tokens[0]
-    x_all = lax.all_gather(x_low, "ctx", axis=0, tiled=True)
+    exchange = (((2, per_seq, d), BF16), ((per_seq, d), BF16), ((per_seq, d), BF16))
+    whole = ((length, d), BF16)
+    x_all, dm_all = linked_call(
+        gather_inputs, 0, (whole, whole), (), 6 * CHUNKS, (x_low, cotangent[0])
+    )
     vec = jnp.concatenate(
         [v[0] for v in (g_one, s_one, b_attend, g_two, s_two, b_contract, b_joint, b_expand)]
     )
@@ -216,7 +442,6 @@
     we = lax.all_to_all(we, "ctx", 0, 0, tiled=True).reshape(nc * own, ff)
     we = lax.all_gather(we, "fsdp", axis=0, tiled=True)
     wc = lax.all_gather(w_contract[0], "fsdp", axis=0, tiled=True)
-    dm_all = lax.all_gather(cotangent[0], "ctx", axis=0, tiled=True)
 
     normed, joint, mix, logsum, part = local_call(
         functools.partial(attend_fwd, head),
@@ -232,11 +457,14 @@
         12 * length * d,
         (x_all, g1, s1, bj, wj, wo),
     )
-    x = x_low.astype(F32)
-    mixed = lax.psum_scatter(part, "ctx", scatter_dimension=0, tiled=True).astype(F32)
-    x1 = x + (mixed + ba)
-    h2 = norm_apply(x1, g2, s2).astype(BF16)
-    h2_all = lax.all_gather(h2, "ctx", axis=0, tiled=True)
+    x1, h2_all = linked_call(
+        between_forward,
+        1,
+        (((per_seq, d), F32), whole),
+        exchange,
+        6 * CHUNKS,
+        (part, x_low, ba, g2, s2),
+    )
 
     down, dh2, d_up, d_down, d_be = local_call(
         feed_both,
@@ -252,14 +480,15 @@
         18 * length * d,
         (h2_all, dm_all, we, be, wc),
     )
-    dh2 = lax.psum_scatter(dh2, "ctx", scatter_dimension=0, tiled=True).astype(F32)
-    dx = cotangent[0].astype(F32)
-    back, d_g2, d_s2 = norm_back(x1, g2, dh2)
-    dx1 = dx + back
-    da = dx1.astype(BF16)
-    da_all = lax.all_gather(da, "ctx", axis=0, tiled=True)
-    down = lax.psum_scatter(down, "ctx", scatter_dimension=0, tiled=True).astype(F32)
-    block_out = (x1 + (down + bc)).astype(BF16)
+    row = ((1, d), F32)
+    dx1, da_all, d_g2, d_s2, d_ba = linked_call(
+        between_backward,
+        2,
+        (((per_seq, d), F32), whole, row, row, row),
+        exchange,
+        6 * CHUNKS,
+        (dh2, x1, cotangent[0], g2),
+    )
 
     d_wo, d_wj, sums, dh1 = local_call(
         functools.partial(attend_bwd, head),
@@ -278,13 +507,22 @@
         12 * length * d,
         (da_all, wo, mix, joint, logsum, normed, wj),
     )
-    dh1 = lax.psum_scatter(dh1, "ctx", scatter_dimension=0, tiled=True).astype(F32)
-    back, d_g1, d_s1 = norm_back(x, g1, dh1)
-    grad_tokens = dx1 + back
-
+    (block_out,) = linked_call(
+        sum_block, 3, (((per_seq, d), BF16),), exchange, 3 * CHUNKS, (down, x1, bc)
+    )
     out_wc = lax.psum_scatter(d_down, "fsdp", scatter_dimension=0, tiled=True)
+    out_we = lax.psum_scatter(d_up, "fsdp", scatter_dimension=0, tiled=True)
+    dh1, block_out, out_wc, out_we = lax.optimization_barrier((dh1, block_out, out_wc, out_we))
+    grad_tokens, d_g1, d_s1 = linked_call(
+        sum_grad,
+        4,
+        (((per_seq, d), F32), row, row),
+        exchange,
+        3 * CHUNKS,
+        (dh1, x_low, g1, dx1),
+    )
+
     out_wc = swap_sum(out_wc, replicas)
-    out_we = lax.psum_scatter(d_up, "fsdp", scatter_dimension=0, tiled=True)
     out_we = lax.all_to_all(out_we.reshape(nc, own, ff), "ctx", 0, 0, tiled=True)
     out_we = out_we.reshape(nc, own, nf, part_ff).transpose(1, 2, 0, 3).reshape(own, nf * nc * part_ff)
     out_we = swap_sum(out_we, replicas)
@@ -292,8 +530,7 @@
     out_wo = lax.ppermute(out_wo, ("fsdp", "ctx"), [(b, a) for a, b in turn])
     out_wo = swap_sum(out_wo, replicas)
 
-    d_ba = jnp.sum(da.astype(F32), axis=0)
-    d_bc = jnp.sum(dx, axis=0)
+    d_bc = jnp.sum(cotangent[0].astype(F32), axis=0)
     mine = (jnp.arange(nc) == at_c).astype(F32)
     sums = sums.reshape(3, 1, width)
     d_bj = jnp.stack([sums[0], sums[2]]) * mine[None, :, None]

time: 518 us -> 283 us (0.55)
  waiting for transfers between devices: 352 us -> 30.9 us
  Pallas kernels: 39.6 us -> 135 us
  blocking collectives: 56.1 us -> 27.4 us
  starting transfers between devices: 13.3 us -> 29 us
  local copies, waits for them, and re-layouts: 23.4 us -> 38.9 us
  other arithmetic: 18.1 us -> 6.66 us
    reduce_scatter x4 -> x0, waiting for transfers between devices: 97.6 us -> none  [the longest x1 30.7 us: on_device(): lax.psum_scatter(dh2, 'ctx', scatter_dimension=0, tiled=True).astype(F32)]
    pallas_call x0 -> x5, Pallas kernels: none -> 94.9 us  [linked_call(): pl.pallas_call(body, out_shape=tuple((jax.ShapeDtypeStruct(shape, kind) f...]
    all_gather x4 -> x0, waiting for transfers between devices: 78.8 us -> none  [the longest x1 21.9 us: on_device(): h2_all = lax.all_gather(h2, 'ctx', axis=0, tiled=True)]
    all_gather x1, waiting for transfers between devices: 31.1 us -> 1.07 us  [on_device(): we = lax.all_gather(we, 'fsdp', axis=0, tiled=True)]
    reduce_scatter x1, waiting for transfers between devices: 28.8 us -> 0.02 us  [on_device(): out_we = lax.psum_scatter(d_up, 'fsdp', scatter_dimension=0, tiled=True)]
    all_gather x1, waiting for transfers between devices: 28 us -> 0.01 us  [on_device(): wc = lax.all_gather(w_contract[0], 'fsdp', axis=0, tiled=True)]
    reduce_scatter x1, waiting for transfers between devices: 27.2 us -> 0.02 us  [on_device(): out_wc = lax.psum_scatter(d_down, 'fsdp', scatter_dimension=0, tiled=True)]
    all_to_all x2 -> x0, blocking collectives: 19.3 us -> none  [the longest x1 9.81 us: on_device(): lax.all_to_all(out_we.reshape(nc, own, ff), 'ctx', 0, 0, tiled=True)]
  transfers between devices with their start and end apart: 23 -> 17, of which waited for: 18 -> 6; matrix products, arithmetic and copies ran while one was open for 4% -> 5% of each run, Pallas kernels for 0% -> 43%
where the time goes in v2:
time: 283 us; the launch traced here: 282 us
  Pallas kernels  135 us (48%)
  local copies, waits for them, and re-layouts  38.9 us (14%)
  waiting for transfers between devices  30.9 us (11%)
  starting transfers between devices  29 us (10%)
  blocking collectives  27.4 us (10%)
  between operations  14.6 us (5%)
  other arithmetic  6.66 us (2%)
    pallas_call x5, Pallas kernels, linked_call(): pl.pallas_call(body, out_shape=tuple((jax.ShapeDtypeStruct(shape, kind) f...  94.9 us
    pallas_call x3, Pallas kernels, local_call(): pl.pallas_call(body, out_shape=tuple((jax.ShapeDtypeStruct(shape, kind) f...  40.1 us
    unnamed x56, local copies, waits for them, and re-layouts  24.1 us
    all_gather x1, blocking collectives, on_device(): wo = lax.all_gather(wo, 'fsdp', axis=0, tiled=True)  16.5 us
    all_to_all x1, blocking collectives, on_device(): block = lax.all_to_all(block, 'ctx', 0, 0, tiled=True)  10.9 us
    reduce_scatter x1, waiting for transfers between devices, on_device(): tail = lax.psum_scatter(tail, 'fsdp', scatter_dimension=0, tiled=True)  9.67 us
    all_to_all x1, starting transfers between devices, on_device(): lax.all_to_all(out_we.reshape(nc, own, ff), 'ctx', 0, 0, tiled=True)  9.48 us
    all_to_all x1, starting transfers between devices, on_device(): we = lax.all_to_all(we, 'ctx', 0, 0, tiled=True).reshape(nc * own, ff)  7.67 us
  transfers between devices with their start and end apart: 17, of which 6 were waited for; matrix products, arithmetic and copies ran while one was open for 5% of the time, Pallas kernels for 43%

profile of v2, /device:TPU:0, one launch (start us, length us, event | category | flops | bytes accessed | tf_op | source)
XLA Modules:
  0.0 282.4 jit_solution(4449061298094397334)
XLA Ops:
  7.9 4.8 %concatenate.39 = bf16[576]{0:T(1024)(128)(2,1)S(1)} concatenate(bf16[48]{0:T(256)(128)(2,1)} %bitcast.67, bf16[48]{0:T(256)(128)(2,1)} %bitcast.68, bf16[48]{0:T(256)(128)(2,1)} %bitcast.69, bf16[48]{0:T(256)(128)(2,1)} %bitcast.70, bf16[48]{0:T(256)(128)(2,1)} %bitcast.71, bf16[48]{0:T(256)(128)(2,1)} %bitcast.72, bf16[96]{0:T(256)(128)(2,1)} %bitcast.73, bf16[192]{0:T(256)(128)(2,1)S(1)} %reduce.4), dimensions={0} | concatenate | bytes 2304 | tf_op jit(solution)/shard_map/concatenate | solution.py:420
  14.5 10.9 %all_to_all.20 = bf16[4,64,576]{2,1,0:T(8,128)(2,1)} all-to-all(bf16[4,64,576]{2,1,0:T(8,128)(2,1)S(1)} %pad_maximum_fusion), channel_id=1, replica_groups=mesh['rep'=2,'fsdp'=4,'ctx'=4] {'ctx'}, dimensions={0} | all-to-all | bytes 589824 | tf_op jit(solution)/shard_map/all_to_all | solution.py:428
  28.6 7.7 %all-to-all-start.1 = ((bf16[4,48,768]{2,1,0:T(8,128)(2,1)}), bf16[4,48,768]{2,1,0:T(8,128)(2,1)S(1)}, u32[]{:S(2)}, u32[]{:S(2)}) async-start(bf16[4,48,768]{2,1,0:T(8,128)(2,1)} %reshape.298), calls=%async_computation.1 | async-start | bytes 589824 | tf_op jit(solution)/shard_map/all_to_all | solution.py:442
  36.3 25.0 %shard_map.245 = (bf16[1024,768]{1,0:T(8,128)(2,1)S(1)}, bf16[1024,768]{1,0:T(8,128)(2,1)S(1)}) custom-call(bf16[256,768]{1,0:T(8,128)(2,1)S(1)} %bitcast.54, bf16[256,768]{1,0:T(8,128)(2,1)S(1)} %bitcast.50), custom_call_target="tpu_custom_call" | custom-call | flops 10000000000 | bytes 40000000 | tf_op jit(solution)/shard_map/pallas_call | solution.py:360
  63.6 16.5 %all_gather.13.w_out = bf16[192,768]{1,0:T(8,128)(2,1)S(1)} all-gather(bf16[48,768]{1,0:T(8,128)(2,1)S(1)} %collective-permute-done), channel_id=1, replica_groups=mesh['rep'=2,'fsdp'=4,'ctx'=4] {'fsdp'}, dimensions={0}, use_global_device_ids=true | all-gather | bytes 368640 | tf_op jit(solution)/shard_map/all_gather | solution.py:440
  83.0 1.3 slice.110
  84.3 11.2 %shard_map.246 = (bf16[1024,768]{1,0:T(8,128)(2,1)S(1)}, bf16[1024,576]{1,0:T(8,128)(2,1)S(1)}, bf16[1024,192]{1,0:T(8,128)(2,1)S(1)}, f32[1024,128]{1,0:T(8,128)S(1)}, bf16[1024,768]{1,0:T(8,128)(2,1)}) custom-call(bf16[1024,768]{1,0:T(8,128)(2,1)} %copy-done.4, f32[1,768]{1,0:T(1,128)S(1)} %reshape.290.gain, f32[1,768]{1,0:T(1,128)S(1)} %reshape.291.shift, ...), custom_call_target="tpu_custom_call" | custom-call | flops 2013265920 | bytes 9437184 | tf_op jit(solution)/shard_map/pallas_call | solution.py:143
  97.7 1.6 copy-done.6
  99.3 21.9 %shard_map.247 = (f32[256,768]{1,0:T(8,128)S(1)}, bf16[1024,768]{1,0:T(8,128)(2,1)S(1)}) custom-call(bf16[1024,768]{1,0:T(8,128)(2,1)S(1)} %copy-done.6, bf16[256,768]{1,0:T(8,128)(2,1)S(1)} %bitcast.55, f32[1,768]{1,0:T(1,128)S(1)} %reshape.295.bias, f32[1,768]{1,0:T(1,128)S(1)} %reshape.296.gain, f32[1,768]{1,0:T(1,128)S(1)} %reshape.297.shift), custom_call_target="tpu_custom_call" | custom-call | flops 10000000000 | bytes 40000000 | tf_op jit(solution)/shard_map/pallas_call | solution.py:360
  124.4 1.3 copy-done.1
  125.7 1.3 copy-done.2
  126.9 12.3 %shard_map.248 = (bf16[1024,768]{1,0:T(8,128)(2,1)}, bf16[1024,768]{1,0:T(8,128)(2,1)}, bf16[768,768]{1,0:T(8,128)(2,1)}, bf16[768,768]{1,0:T(8,128)(2,1)}, f32[1,768]{1,0:T(1,128)S(1)}) custom-call(bf16[1024,768]{1,0:T(8,128)(2,1)} %copy-done.16, bf16[1024,768]{1,0:T(8,128)(2,1)} %copy-done.13, bf16[768,768]{1,0:T(8,128)(2,1)S(1)} %copy-done.2, ...), custom_call_target="tpu_custom_call" | custom-call | flops 7247757312 | bytes 14155776 | tf_op jit(solution)/shard_map/pallas_call | solution.py:143
  139.9 1.4 copy-done.15
  142.4 22.4 %shard_map.249 = (f32[256,768]{1,0:T(8,128)S(1)}, bf16[1024,768]{1,0:T(8,128)(2,1)S(1)}, f32[1,768]{1,0:T(1,128)S(1)}, f32[1,768]{1,0:T(1,128)S(1)}, f32[1,768]{1,0:T(1,128)S(1)}) custom-call(bf16[1024,768]{1,0:T(8,128)(2,1)S(1)} %copy-done.15, f32[256,768]{1,0:T(8,128)S(1)} %copy-done.18, bf16[256,768]{1,0:T(8,128)(2,1)S(1)} %bitcast.51, ...), custom_call_target="tpu_custom_call" | custom-call | flops 10000000000 | bytes 40000000 | tf_op jit(solution)/shard_map/pallas_call | solution.py:360
  167.0 1.3 copy-done.8
  169.4 16.7 %shard_map.250 = (bf16[192,768]{1,0:T(8,128)(2,1)}, bf16[768,576]{1,0:T(8,128)(2,1)S(1)}, f32[1,576]{1,0:T(1,128)S(1)}, bf16[1024,768]{1,0:T(8,128)(2,1)}) custom-call(bf16[1024,768]{1,0:T(8,128)(2,1)} %copy-done.12, bf16[192,768]{1,0:T(8,128)(2,1)S(1)} %all_gather.13.w_out, bf16[1024,192]{1,0:T(8,128)(2,1)S(1)} %get-tuple-element.51.mix, ...), custom_call_target="tpu_custom_call" | custom-call | flops 4429185024 | bytes 9437184 | tf_op jit(solution)/shard_map/pallas_call | solution.py:143
  186.5 1.4 copy-done.14
  189.1 12.9 %shard_map.251 = bf16[256,768]{1,0:T(8,128)(2,1)S(1)} custom-call(bf16[1024,768]{1,0:T(8,128)(2,1)S(1)} %copy-done.14, f32[256,768]{1,0:T(8,128)S(1)} %copy-done.19, f32[1,768]{1,0:T(1,128)S(1)} %reshape.302.bias), custom_call_target="tpu_custom_call" | custom-call | flops 10000000000 | bytes 40000000 | tf_op jit(solution)/shard_map/pallas_call | solution.py:360
  202.2 1.4 copy-done.11
  203.5 12.7 %shard_map.252 = (f32[256,768]{1,0:T(8,128)S(1)}, f32[1,768]{1,0:T(1,128)S(1)}, f32[1,768]{1,0:T(1,128)S(1)}) custom-call(bf16[1024,768]{1,0:T(8,128)(2,1)S(1)} %copy-done.11, bf16[256,768]{1,0:T(8,128)(2,1)S(1)} %bitcast.56, f32[1,768]{1,0:T(1,128)S(1)} %reshape.290.gain, f32[256,768]{1,0:T(8,128)S(1)} %copy-done.21), custom_call_target="tpu_custom_call" | custom-call | flops 10000000000 | bytes 40000000 | tf_op jit(solution)/shard_map/pallas_call | solution.py:360
  216.6 1.3 fusion.1
  217.9 3.3 %reduce-scatter.11.cloned.1.call-done = bf16[48,768]{1,0:T(8,128)(2,1)} async-done(((bf16[192,768]{1,0:T(8,128)(2,1)}), bf16[48,768]{1,0:T(8,128)(2,1)}) %reduce-scatter.11.cloned.1.call-update) | async-done | bytes 73744 | tf_op jit(solution)/shard_map/reduce_scatter | solution.py:529
  221.2 1.5 collective-permute-start.3
  222.7 1.5 collective-permute-start.4
  224.7 9.5 %all-to-all-start.3 = ((bf16[4,48,768]{2,1,0:T(8,128)(2,1)}), bf16[4,48,768]{2,1,0:T(8,128)(2,1)S(1)}, u32[]{:S(2)}, u32[]{:S(2)}) async-start(bf16[4,48,768]{2,1,0:T(8,128)(2,1)} %bitcast.27), calls=%async_computation.7 | async-start | bytes 589824 | tf_op jit(solution)/shard_map/all_to_all | solution.py:526
  234.9 5.7 %all-to-all-done.3 = bf16[4,48,768]{2,1,0:T(8,128)(2,1)S(1)} async-done(((bf16[4,48,768]{2,1,0:T(8,128)(2,1)}), bf16[4,48,768]{2,1,0:T(8,128)(2,1)S(1)}, u32[]{:S(2)}, u32[]{:S(2)}) %all-to-all-start.3) | async-done | bytes 294944 | tf_op jit(solution)/shard_map/all_to_all | solution.py:526
  241.8 1.6 collective-permute-start.5
  243.3 9.7 %reduce-scatter.9.cloned.1.call-done = bf16[4,64,576]{2,1,0:T(8,128)(2,1)} async-done(((bf16[16,64,576]{2,1,0:T(8,128)(2,1)}), bf16[4,64,576]{2,1,0:T(8,128)(2,1)}) %reduce-scatter.9.cloned.1.call-update) | async-done | bytes 294928 | tf_op jit(solution)/shard_map/reduce_scatter | solution.py:546
  253.0 3.5 %all-to-all-start.2 = ((bf16[4,64,576]{2,1,0:T(8,128)(2,1)}), bf16[4,64,576]{2,1,0:T(8,128)(2,1)S(1)}, u32[]{:S(2)}, u32[]{:S(2)}) async-start(bf16[4,64,576]{2,1,0:T(8,128)(2,1)} %reduce-scatter.9.cloned.1.call-done), calls=%async_computation.5 | async-start | bytes 655360 | tf_op jit(solution)/shard_map/all_to_all | solution.py:547
  257.3 5.8 %all-to-all-done.2 = bf16[4,64,576]{2,1,0:T(8,128)(2,1)S(1)} async-done(((bf16[4,64,576]{2,1,0:T(8,128)(2,1)}), bf16[4,64,576]{2,1,0:T(8,128)(2,1)S(1)}, u32[]{:S(2)}, u32[]{:S(2)}) %all-to-all-start.2) | async-done | bytes 294944 | tf_op jit(solution)/shard_map/all_to_all | solution.py:547
  263.2 1.6 collective-permute-start.1
  268.7 4.4 %collective-permute-done.2 = bf16[48,2304]{1,0:T(8,128)(2,1)S(1)} collective-permute-done((bf16[48,2304]{1,0:T(8,128)(2,1)S(1)}, bf16[48,2304]{1,0:T(8,128)(2,1)S(1)}, u32[]{:S(2)}, u32[]{:S(2)}) %collective-permute-start.2) | collective-permute-done | bytes 221216 | tf_op jit(solution)/shard_map/ppermute | solution.py:381
  (147 shorter events, 32.8 us)
Async XLA Ops:
  7.2 73.9 %all-gather.5.cloned.1.call-start = ((), (), s32[]{:S(2)}) async-start(), calls=%async_computation.8 | async-start | bytes 1638400 | tf_op jit(solution)/shard_map/all_gather | solution.py:429
  13.9 12.2 %copy-start.25 = (bf16[1,48,768]{2,1,0:T(8,128)(2,1)S(1)}, bf16[1,48,768]{2,1,0:T(8,128)(2,1)}, u32[]{:S(2)}) copy-start(bf16[1,48,768]{2,1,0:T(8,128)(2,1)} %param.19) | copy-start | bytes 221188
  13.9 12.9 %copy-start.23 = (bf16[1,48,3072]{2,1,0:T(8,128)(2,1)S(1)}, bf16[1,48,3072]{2,1,0:T(8,128)(2,1)}, u32[]{:S(2)}) copy-start(bf16[1,48,3072]{2,1,0:T(8,128)(2,1)} %param.23) | copy-start | bytes 884740
  25.4 10.9 %copy-start = (bf16[1,256,768]{2,1,0:T(8,128)(2,1)S(1)}, bf16[1,256,768]{2,1,0:T(8,128)(2,1)}, u32[]{:S(2)}) copy-start(bf16[1,256,768]{2,1,0:T(8,128)(2,1)} %param.27) | copy-start | bytes 1179652
  25.4 10.8 %copy-start.3 = (bf16[1,256,768]{2,1,0:T(8,128)(2,1)S(1)}, bf16[1,256,768]{2,1,0:T(8,128)(2,1)}, u32[]{:S(2)}) copy-start(bf16[1,256,768]{2,1,0:T(8,128)(2,1)} %param.14) | copy-start | bytes 1179652
  25.4 97.9 %all-gather.9.cloned.1.call-start = ((), (), s32[]{:S(2)}) async-start(), calls=%async_computation.14 | async-start | bytes 1474560 | tf_op jit(solution)/shard_map/all_gather | solution.py:444
  26.2 37.4 %collective-permute-start = (bf16[48,768]{1,0:T(8,128)(2,1)S(1)}, bf16[48,768]{1,0:T(8,128)(2,1)S(1)}, u32[]{:S(2)}, u32[]{:S(2)}) collective-permute-start(bf16[48,768]{1,0:T(8,128)(2,1)S(1)} %bitcast.74), channel_id=1, source_target_pairs={{0,0},{1,4},{2,8},{3,12},{4,1},{5,5},{6,9},{7,13},{8,2},{9,6},{10,... | collective-permute-start | bytes 221192 | tf_op jit(solution)/shard_map/ppermute | solution.py:439
  28.6 51.6 %all-to-all-start.1 = ((bf16[4,48,768]{2,1,0:T(8,128)(2,1)}), bf16[4,48,768]{2,1,0:T(8,128)(2,1)S(1)}, u32[]{:S(2)}, u32[]{:S(2)}) async-start(bf16[4,48,768]{2,1,0:T(8,128)(2,1)} %reshape.298), calls=%async_computation.1 | async-start | bytes 589824 | tf_op jit(solution)/shard_map/all_to_all | solution.py:442
  36.2 88.1 %all-gather.7.cloned.1.call-start = ((), (), s32[]{:S(2)}) async-start(), calls=%async_computation.9 | async-start | bytes 1474560 | tf_op jit(solution)/shard_map/all_gather | solution.py:443
  61.2 1.2 copy-start.4
  80.9 121.2 %reduce-scatter.5.cloned.1.call-start = ((), (), s32[]{:S(2)}) async-start(), calls=%async_computation.10 | async-start | bytes 1474560 | tf_op jit(solution)/shard_map/reduce_scatter | solution.py:513
  97.7 23.5 %copy-start.9 = (f32[1024,128]{1,0:T(8,128)}, f32[1024,128]{1,0:T(8,128)S(1)}, u32[]{:S(2)}) copy-start(f32[1024,128]{1,0:T(8,128)S(1)} %get-tuple-element.53.logsum) | copy-start | bytes 1572868
  97.7 1.6 copy-start.6
  124.4 1.3 copy-start.1
  125.7 1.3 copy-start.2
  139.2 62.9 %reduce-scatter.7.cloned.1.call-start = ((), (), s32[]{:S(2)}) async-start(), calls=%async_computation.11 | async-start | bytes 1474560 | tf_op jit(solution)/shard_map/reduce_scatter | solution.py:514
  139.8 81.4 %reduce-scatter.11.cloned.1.call-start = ((), (), s32[]{:S(2)}) async-start(), calls=%async_computation.13 | async-start | bytes 368640 | tf_op jit(solution)/shard_map/reduce_scatter | solution.py:529
  139.9 1.4 copy-start.15
  167.0 1.3 copy-start.8
  186.5 1.4 copy-start.14
  189.1 13.1 %copy-start.21 = (f32[256,768]{1,0:T(8,128)S(1)}, f32[256,768]{1,0:T(8,128)}, u32[]{:S(2)}) copy-start(f32[256,768]{1,0:T(8,128)} %copy-done.20) | copy-start | bytes 2359300
  202.0 51.0 %reduce-scatter.9.cloned.1.call-start = ((), (), s32[]{:S(2)}) async-start(), calls=%async_computation.12 | async-start | bytes 1638400 | tf_op jit(solution)/shard_map/reduce_scatter | solution.py:546
  202.1 1.4 copy-start.11
  216.6 7.6 %copy-start.24 = (bf16[192,768]{1,0:T(8,128)(2,1)S(1)}, bf16[192,768]{1,0:T(8,128)(2,1)}, u32[]{:S(2)}) copy-start(bf16[192,768]{1,0:T(8,128)(2,1)} %reduce-scatter.5.cloned.1.call-done) | copy-start | bytes 884740
  221.2 1.5 collective-permute-start.3
  222.7 11.5 %collective-permute-start.4 = (bf16[48,768]{1,0:T(8,128)(2,1)S(1)}, bf16[48,768]{1,0:T(8,128)(2,1)S(1)}, u32[]{:S(2)}, u32[]{:S(2)}) collective-permute-start(bf16[48,768]{1,0:T(8,128)(2,1)S(1)} %collective-permute-done.3), channel_id=1, source_target_pairs={{0,16},{16,0},{1,17},{17,1},{2,18},{18,2},{3,19},{19,3},{4,20},{20... | collective-permute-start | bytes 221192 | tf_op jit(solution)/shard_map/ppermute | solution.py:381
  224.2 32.3 %collective-permute-start.6 = (bf16[192,768]{1,0:T(8,128)(2,1)S(1)}, bf16[192,768]{1,0:T(8,128)(2,1)S(1)}, u32[]{:S(2)}, u32[]{:S(2)}) collective-permute-start(bf16[192,768]{1,0:T(8,128)(2,1)S(1)} %copy-done.24), channel_id=1, source_target_pairs={{0,16},{16,0},{1,17},{17,1},{2,18},{18,2},{3,19},{19,3},{4,20},{20... | collective-permute-start | bytes 884744 | tf_op jit(solution)/shard_map/ppermute | solution.py:381
  224.7 15.9 %all-to-all-start.3 = ((bf16[4,48,768]{2,1,0:T(8,128)(2,1)}), bf16[4,48,768]{2,1,0:T(8,128)(2,1)S(1)}, u32[]{:S(2)}, u32[]{:S(2)}) async-start(bf16[4,48,768]{2,1,0:T(8,128)(2,1)} %bitcast.27), calls=%async_computation.7 | async-start | bytes 589824 | tf_op jit(solution)/shard_map/all_to_all | solution.py:526
  241.8 23.0 %collective-permute-start.5 = (bf16[48,3072]{1,0:T(8,128)(2,1)S(1)}, bf16[48,3072]{1,0:T(8,128)(2,1)S(1)}, u32[]{:S(2)}, u32[]{:S(2)}) collective-permute-start(bf16[48,3072]{1,0:T(8,128)(2,1)S(1)} %reshape.308), channel_id=1, source_target_pairs={{0,16},{16,0},{1,17},{17,1},{2,18},{18,2},{3,19},{19,3},{4,20},{20... | collective-permute-start | bytes 884744 | tf_op jit(solution)/shard_map/ppermute | solution.py:381
  253.0 10.2 %all-to-all-start.2 = ((bf16[4,64,576]{2,1,0:T(8,128)(2,1)}), bf16[4,64,576]{2,1,0:T(8,128)(2,1)S(1)}, u32[]{:S(2)}, u32[]{:S(2)}) async-start(bf16[4,64,576]{2,1,0:T(8,128)(2,1)} %reduce-scatter.9.cloned.1.call-done), calls=%async_computation.5 | async-start | bytes 655360 | tf_op jit(solution)/shard_map/all_to_all | solution.py:547
  263.2 3.8 %collective-permute-start.1 = (bf16[1,576]{1,0:T(2,128)(2,1)S(1)}, bf16[1,576]{1,0:T(2,128)(2,1)S(1)}, u32[]{:S(2)}, u32[]{:S(2)}) collective-permute-start(bf16[1,576]{1,0:T(2,128)(2,1)S(1)} %convert_element_type.88), channel_id=1, source_target_pairs={{0,16},{16,0},{1,17},{17,1},{2,18},{18,2},{3,19},{19,3},{4,20},{20... | collective-permute-start | bytes 3464 | tf_op jit(solution)/shard_map/ppermute | solution.py:381
  266.4 6.8 %collective-permute-start.2 = (bf16[48,2304]{1,0:T(8,128)(2,1)S(1)}, bf16[48,2304]{1,0:T(8,128)(2,1)S(1)}, u32[]{:S(2)}, u32[]{:S(2)}) collective-permute-start(bf16[48,2304]{1,0:T(8,128)(2,1)S(1)} %reshape.305), channel_id=1, source_target_pairs={{0,16},{16,0},{1,17},{17,1},{2,18},{18,2},{3,19},{19,3},{4,20},{20... | collective-permute-start | bytes 663560 | tf_op jit(solution)/shard_map/ppermute | solution.py:381
  (11 other events, 11.5 us)
Sparse Core Ops, SparseCore 0:
  25.5 33.3 all-gather.4
  60.5 32.6 all-gather.8
  95.3 29.0 all-gather.6
  139.3 28.2 reduce-scatter.4
  169.8 27.8 reduce-scatter.6
  202.1 18.9 reduce-scatter.10
  223.5 29.4 reduce-scatter.8

commit v3 on v2

--- a/solution.py
+++ b/solution.py
@@ -436,8 +436,21 @@
     be = vecs[:, 8 * own :].reshape(nf, nc, part_ff)
     be = lax.dynamic_index_in_dim(be, at_c, 1, keepdims=False).reshape(1, ff)
 
-    wo = lax.ppermute(w_attend[0], ("fsdp", "ctx"), turn)
-    wo = lax.all_gather(wo, "fsdp", axis=0, tiled=True)
+    if nf == nc:
+        pieces = [
+            lax.ppermute(
+                w_attend[0],
+                ("fsdp", "ctx"),
+                [(c * nc + (f + j) % nc, f * nc + c) for f in range(nf) for c in range(nc)],
+            )
+            for j in range(nc)
+        ]
+        wo = jnp.zeros((width, d), BF16)
+        for j, piece in enumerate(pieces):
+            wo = lax.dynamic_update_slice_in_dim(wo, piece, lax.rem(at_f + j, nc) * own, 0)
+    else:
+        wo = lax.ppermute(w_attend[0], ("fsdp", "ctx"), turn)
+        wo = lax.all_gather(wo, "fsdp", axis=0, tiled=True)
     we = w_expand[0].reshape(own, nf, nc, part_ff).transpose(2, 0, 1, 3).reshape(nc, own, ff)
     we = lax.all_to_all(we, "ctx", 0, 0, tiled=True).reshape(nc * own, ff)
     we = lax.all_gather(we, "fsdp", axis=0, tiled=True)

time: 283 us -> 283 us (level)
  blocking collectives: 27.4 us -> 10.9 us
  waiting for transfers between devices: 30.9 us -> 44.7 us
    all_gather x1 -> x0, blocking collectives: 16.5 us -> none  [on_device(): wo = lax.all_gather(wo, 'fsdp', axis=0, tiled=True)]
    all_gather x1, waiting for transfers between devices: 1.07 us -> 14.9 us  [on_device(): we = lax.all_gather(we, 'fsdp', axis=0, tiled=True)]
    ppermute x1 -> x4, starting transfers between devices: 0.67 us -> 4.84 us  [on_device(): lax.ppermute(w_attend[0], ('fsdp', 'ctx'), [(c * nc + (f + j) % nc, f * n...]
  transfers between devices with their start and end apart: 17 -> 20, of which waited for: 6 -> 6; matrix products, arithmetic and copies ran while one was open for 5% -> 5% of each run, Pallas kernels for 43% -> 44%
where the time goes in v3:
time: 283 us; the launch traced here: 282 us
  Pallas kernels  135 us (48%)
  waiting for transfers between devices  44.7 us (16%)
  local copies, waits for them, and re-layouts  39 us (14%)
  starting transfers between devices  30.9 us (11%)
  between operations  14.6 us (5%)
  blocking collectives  10.9 us (4%)
  other arithmetic  6.65 us (2%)
    pallas_call x5, Pallas kernels, linked_call(): pl.pallas_call(body, out_shape=tuple((jax.ShapeDtypeStruct(shape, kind) f...  95.1 us
    pallas_call x3, Pallas kernels, local_call(): pl.pallas_call(body, out_shape=tuple((jax.ShapeDtypeStruct(shape, kind) f...  40.1 us
    unnamed x56, local copies, waits for them, and re-layouts  24.1 us
    all_gather x1, waiting for transfers between devices, on_device(): we = lax.all_gather(we, 'fsdp', axis=0, tiled=True)  14.9 us
    all_to_all x1, blocking collectives, on_device(): block = lax.all_to_all(block, 'ctx', 0, 0, tiled=True)  10.9 us
    reduce_scatter x1, waiting for transfers between devices, on_device(): tail = lax.psum_scatter(tail, 'fsdp', scatter_dimension=0, tiled=True)  9.71 us
    all_to_all x1, starting transfers between devices, on_device(): lax.all_to_all(out_we.reshape(nc, own, ff), 'ctx', 0, 0, tiled=True)  9.48 us
    all_to_all x1, waiting for transfers between devices, on_device(): tail = lax.all_to_all(tail, 'ctx', 0, 0, tiled=True)  5.82 us
  transfers between devices with their start and end apart: 20, of which 6 were waited for; matrix products, arithmetic and copies ran while one was open for 5% of the time, Pallas kernels for 44%

profile of v3, /device:TPU:0, one launch (start us, length us, event | category | flops | bytes accessed | tf_op | source)
XLA Modules:
  0.0 282.0 jit_solution(14108581099541903128)
XLA Ops:
  7.9 4.8 %concatenate.39 = bf16[576]{0:T(1024)(128)(2,1)S(1)} concatenate(bf16[48]{0:T(256)(128)(2,1)} %bitcast.67, bf16[48]{0:T(256)(128)(2,1)} %bitcast.68, bf16[48]{0:T(256)(128)(2,1)} %bitcast.69, bf16[48]{0:T(256)(128)(2,1)} %bitcast.70, bf16[48]{0:T(256)(128)(2,1)} %bitcast.71, bf16[48]{0:T(256)(128)(2,1)} %bitcast.72, bf16[96]{0:T(256)(128)(2,1)} %bitcast.73, bf16[192]{0:T(256)(128)(2,1)S(1)} %reduce.4), dimensions={0} | concatenate | bytes 2304 | tf_op jit(solution)/shard_map/concatenate | solution.py:420
  14.5 10.9 %all_to_all.20 = bf16[4,64,576]{2,1,0:T(8,128)(2,1)} all-to-all(bf16[4,64,576]{2,1,0:T(8,128)(2,1)S(1)} %pad_maximum_fusion), channel_id=1, replica_groups=mesh['rep'=2,'fsdp'=4,'ctx'=4] {'ctx'}, dimensions={0} | all-to-all | bytes 589824 | tf_op jit(solution)/shard_map/all_to_all | solution.py:428
  26.2 2.0 collective-permute-start.3
  32.7 5.4 %all-to-all-start.1 = ((bf16[4,48,768]{2,1,0:T(8,128)(2,1)}), bf16[4,48,768]{2,1,0:T(8,128)(2,1)S(1)}, u32[]{:S(2)}, u32[]{:S(2)}) async-start(bf16[4,48,768]{2,1,0:T(8,128)(2,1)} %reshape.298), calls=%async_computation.1 | async-start | bytes 589824 | tf_op jit(solution)/shard_map/all_to_all | solution.py:455
  38.2 24.6 %shard_map.245 = (bf16[1024,768]{1,0:T(8,128)(2,1)S(1)}, bf16[1024,768]{1,0:T(8,128)(2,1)S(1)}) custom-call(bf16[256,768]{1,0:T(8,128)(2,1)S(1)} %bitcast.54, bf16[256,768]{1,0:T(8,128)(2,1)S(1)} %bitcast.50), custom_call_target="tpu_custom_call" | custom-call | flops 10000000000 | bytes 40000000 | tf_op jit(solution)/shard_map/pallas_call | solution.py:360
  68.1 1.3 slice.110
  69.5 11.2 %shard_map.246 = (bf16[1024,768]{1,0:T(8,128)(2,1)S(1)}, bf16[1024,576]{1,0:T(8,128)(2,1)S(1)}, bf16[1024,192]{1,0:T(8,128)(2,1)S(1)}, f32[1024,128]{1,0:T(8,128)S(1)}, bf16[1024,768]{1,0:T(8,128)(2,1)}) custom-call(bf16[1024,768]{1,0:T(8,128)(2,1)} %copy-done.4, f32[1,768]{1,0:T(1,128)S(1)} %reshape.290.gain, f32[1,768]{1,0:T(1,128)S(1)} %reshape.291.shift, ...), custom_call_target="tpu_custom_call" | custom-call | flops 2013265920 | bytes 9437184 | tf_op jit(solution)/shard_map/pallas_call | solution.py:143
  82.9 1.6 copy-done.6
  84.6 22.4 %shard_map.247 = (f32[256,768]{1,0:T(8,128)S(1)}, bf16[1024,768]{1,0:T(8,128)(2,1)S(1)}) custom-call(bf16[1024,768]{1,0:T(8,128)(2,1)S(1)} %copy-done.6, bf16[256,768]{1,0:T(8,128)(2,1)S(1)} %bitcast.55, f32[1,768]{1,0:T(1,128)S(1)} %reshape.295.bias, f32[1,768]{1,0:T(1,128)S(1)} %reshape.296.gain, f32[1,768]{1,0:T(1,128)S(1)} %reshape.297.shift), custom_call_target="tpu_custom_call" | custom-call | flops 10000000000 | bytes 40000000 | tf_op jit(solution)/shard_map/pallas_call | solution.py:360
  109.1 14.9 %all-gather.7.cloned.1.call-done.w_up = bf16[768,768]{1,0:T(8,128)(2,1)} async-done(((bf16[192,768]{1,0:T(8,128)(2,1)}), bf16[768,768]{1,0:T(8,128)(2,1)}) %all-gather.7.cloned.1.call-update) | async-done | bytes 1179664 | tf_op jit(solution)/shard_map/all_gather | solution.py:456
  123.9 1.3 copy-done.1
  125.2 1.3 copy-done.2
  126.5 12.3 %shard_map.248 = (bf16[1024,768]{1,0:T(8,128)(2,1)}, bf16[1024,768]{1,0:T(8,128)(2,1)}, bf16[768,768]{1,0:T(8,128)(2,1)}, bf16[768,768]{1,0:T(8,128)(2,1)}, f32[1,768]{1,0:T(1,128)S(1)}) custom-call(bf16[1024,768]{1,0:T(8,128)(2,1)} %copy-done.16, bf16[1024,768]{1,0:T(8,128)(2,1)} %copy-done.13, bf16[768,768]{1,0:T(8,128)(2,1)S(1)} %copy-done.2, ...), custom_call_target="tpu_custom_call" | custom-call | flops 7247757312 | bytes 14155776 | tf_op jit(solution)/shard_map/pallas_call | solution.py:143
  139.4 1.4 copy-done.15
  141.9 22.4 %shard_map.249 = (f32[256,768]{1,0:T(8,128)S(1)}, bf16[1024,768]{1,0:T(8,128)(2,1)S(1)}, f32[1,768]{1,0:T(1,128)S(1)}, f32[1,768]{1,0:T(1,128)S(1)}, f32[1,768]{1,0:T(1,128)S(1)}) custom-call(bf16[1024,768]{1,0:T(8,128)(2,1)S(1)} %copy-done.15, f32[256,768]{1,0:T(8,128)S(1)} %copy-done.18, bf16[256,768]{1,0:T(8,128)(2,1)S(1)} %bitcast.51, ...), custom_call_target="tpu_custom_call" | custom-call | flops 10000000000 | bytes 40000000 | tf_op jit(solution)/shard_map/pallas_call | solution.py:360
  166.5 1.3 copy-done.8
  168.9 16.7 %shard_map.250 = (bf16[192,768]{1,0:T(8,128)(2,1)}, bf16[768,576]{1,0:T(8,128)(2,1)S(1)}, f32[1,576]{1,0:T(1,128)S(1)}, bf16[1024,768]{1,0:T(8,128)(2,1)}) custom-call(bf16[1024,768]{1,0:T(8,128)(2,1)} %copy-done.12, bf16[192,768]{1,0:T(8,128)(2,1)S(1)} %constant_dynamic-update-slice_fusion.w_out, bf16[1024,192]{1,0:T(8,128)(2,1)S(1)} %get-tuple-element.51.mix, ...), custom_call_target="tpu_custom_call" | custom-call | flops 4429185024 | bytes 9437184 | tf_op jit(solution)/shard_map/pallas_call | solution.py:143
  186.0 1.4 copy-done.14
  188.6 12.9 %shard_map.251 = bf16[256,768]{1,0:T(8,128)(2,1)S(1)} custom-call(bf16[1024,768]{1,0:T(8,128)(2,1)S(1)} %copy-done.14, f32[256,768]{1,0:T(8,128)S(1)} %copy-done.19, f32[1,768]{1,0:T(1,128)S(1)} %reshape.302.bias), custom_call_target="tpu_custom_call" | custom-call | flops 10000000000 | bytes 40000000 | tf_op jit(solution)/shard_map/pallas_call | solution.py:360
  201.7 1.4 copy-done.11
  203.1 12.7 %shard_map.252 = (f32[256,768]{1,0:T(8,128)S(1)}, f32[1,768]{1,0:T(1,128)S(1)}, f32[1,768]{1,0:T(1,128)S(1)}) custom-call(bf16[1024,768]{1,0:T(8,128)(2,1)S(1)} %copy-done.11, bf16[256,768]{1,0:T(8,128)(2,1)S(1)} %bitcast.56, f32[1,768]{1,0:T(1,128)S(1)} %reshape.290.gain, f32[256,768]{1,0:T(8,128)S(1)} %copy-done.21), custom_call_target="tpu_custom_call" | custom-call | flops 10000000000 | bytes 40000000 | tf_op jit(solution)/shard_map/pallas_call | solution.py:360
  217.4 3.3 %reduce-scatter.11.cloned.1.call-done = bf16[48,768]{1,0:T(8,128)(2,1)} async-done(((bf16[192,768]{1,0:T(8,128)(2,1)}), bf16[48,768]{1,0:T(8,128)(2,1)}) %reduce-scatter.11.cloned.1.call-update) | async-done | bytes 73744 | tf_op jit(solution)/shard_map/reduce_scatter | solution.py:542
  220.7 1.5 collective-permute-start.6
  222.3 1.5 collective-permute-start.7
  224.3 9.5 %all-to-all-start.3 = ((bf16[4,48,768]{2,1,0:T(8,128)(2,1)}), bf16[4,48,768]{2,1,0:T(8,128)(2,1)S(1)}, u32[]{:S(2)}, u32[]{:S(2)}) async-start(bf16[4,48,768]{2,1,0:T(8,128)(2,1)} %bitcast.27), calls=%async_computation.7 | async-start | bytes 589824 | tf_op jit(solution)/shard_map/all_to_all | solution.py:539
  234.4 5.7 %all-to-all-done.3 = bf16[4,48,768]{2,1,0:T(8,128)(2,1)S(1)} async-done(((bf16[4,48,768]{2,1,0:T(8,128)(2,1)}), bf16[4,48,768]{2,1,0:T(8,128)(2,1)S(1)}, u32[]{:S(2)}, u32[]{:S(2)}) %all-to-all-start.3) | async-done | bytes 294944 | tf_op jit(solution)/shard_map/all_to_all | solution.py:539
  241.3 1.5 collective-permute-start.8
  242.8 9.7 %reduce-scatter.9.cloned.1.call-done = bf16[4,64,576]{2,1,0:T(8,128)(2,1)} async-done(((bf16[16,64,576]{2,1,0:T(8,128)(2,1)}), bf16[4,64,576]{2,1,0:T(8,128)(2,1)}) %reduce-scatter.9.cloned.1.call-update) | async-done | bytes 294928 | tf_op jit(solution)/shard_map/reduce_scatter | solution.py:559
  252.5 3.5 %all-to-all-start.2 = ((bf16[4,64,576]{2,1,0:T(8,128)(2,1)}), bf16[4,64,576]{2,1,0:T(8,128)(2,1)S(1)}, u32[]{:S(2)}, u32[]{:S(2)}) async-start(bf16[4,64,576]{2,1,0:T(8,128)(2,1)} %reduce-scatter.9.cloned.1.call-done), calls=%async_computation.5 | async-start | bytes 655360 | tf_op jit(solution)/shard_map/all_to_all | solution.py:560
  256.9 5.8 %all-to-all-done.2 = bf16[4,64,576]{2,1,0:T(8,128)(2,1)S(1)} async-done(((bf16[4,64,576]{2,1,0:T(8,128)(2,1)}), bf16[4,64,576]{2,1,0:T(8,128)(2,1)S(1)}, u32[]{:S(2)}, u32[]{:S(2)}) %all-to-all-start.2) | async-done | bytes 294944 | tf_op jit(solution)/shard_map/all_to_all | solution.py:560
  262.7 1.5 collective-permute-start.4
  268.3 4.4 %collective-permute-done.5 = bf16[48,2304]{1,0:T(8,128)(2,1)S(1)} collective-permute-done((bf16[48,2304]{1,0:T(8,128)(2,1)S(1)}, bf16[48,2304]{1,0:T(8,128)(2,1)S(1)}, u32[]{:S(2)}, u32[]{:S(2)}) %collective-permute-start.5) | collective-permute-done | bytes 221216 | tf_op jit(solution)/shard_map/ppermute | solution.py:381
  (157 shorter events, 35.2 us)
Async XLA Ops:
  7.2 59.1 %all-gather.5.cloned.1.call-start = ((), (), s32[]{:S(2)}) async-start(), calls=%async_computation.8 | async-start | bytes 1638400 | tf_op jit(solution)/shard_map/all_gather | solution.py:429
  13.9 12.2 %copy-start.25 = (bf16[1,48,768]{2,1,0:T(8,128)(2,1)S(1)}, bf16[1,48,768]{2,1,0:T(8,128)(2,1)}, u32[]{:S(2)}) copy-start(bf16[1,48,768]{2,1,0:T(8,128)(2,1)} %param.19) | copy-start | bytes 221188
  13.9 17.1 %copy-start.23 = (bf16[1,48,3072]{2,1,0:T(8,128)(2,1)S(1)}, bf16[1,48,3072]{2,1,0:T(8,128)(2,1)}, u32[]{:S(2)}) copy-start(bf16[1,48,3072]{2,1,0:T(8,128)(2,1)} %param.23) | copy-start | bytes 884740
  25.4 12.8 %copy-start = (bf16[1,256,768]{2,1,0:T(8,128)(2,1)S(1)}, bf16[1,256,768]{2,1,0:T(8,128)(2,1)}, u32[]{:S(2)}) copy-start(bf16[1,256,768]{2,1,0:T(8,128)(2,1)} %param.27) | copy-start | bytes 1179652
  25.4 12.8 %copy-start.3 = (bf16[1,256,768]{2,1,0:T(8,128)(2,1)S(1)}, bf16[1,256,768]{2,1,0:T(8,128)(2,1)}, u32[]{:S(2)}) copy-start(bf16[1,256,768]{2,1,0:T(8,128)(2,1)} %param.14) | copy-start | bytes 1179652
  25.4 83.7 %all-gather.9.cloned.1.call-start = ((), (), s32[]{:S(2)}) async-start(), calls=%async_computation.14 | async-start | bytes 1474560 | tf_op jit(solution)/shard_map/all_gather | solution.py:457
  26.2 39.1 %collective-permute-start.3 = (bf16[48,768]{1,0:T(8,128)(2,1)S(1)}, bf16[48,768]{1,0:T(8,128)(2,1)S(1)}, u32[]{:S(2)}, u32[]{:S(2)}) collective-permute-start(bf16[48,768]{1,0:T(8,128)(2,1)S(1)} %bitcast.74), channel_id=1, source_target_pairs={{3,0},{7,1},{11,2},{15,3},{0,4},{4,5},{8,6},{12,7},{1,8},{5,9},{9,... | collective-permute-start | bytes 221192 | tf_op jit(solution)/shard_map/ppermute | solution.py:441
  28.2 37.0 %collective-permute-start.2 = (bf16[48,768]{1,0:T(8,128)(2,1)S(1)}, bf16[48,768]{1,0:T(8,128)(2,1)S(1)}, u32[]{:S(2)}, u32[]{:S(2)}) collective-permute-start(bf16[48,768]{1,0:T(8,128)(2,1)S(1)} %bitcast.75), channel_id=1, source_target_pairs={{2,0},{6,1},{10,2},{14,3},{3,4},{7,5},{11,6},{15,7},{0,8},{4,9},{8... | collective-permute-start | bytes 221192 | tf_op jit(solution)/shard_map/ppermute | solution.py:441
  29.5 35.7 %collective-permute-start.1 = (bf16[48,768]{1,0:T(8,128)(2,1)S(1)}, bf16[48,768]{1,0:T(8,128)(2,1)S(1)}, u32[]{:S(2)}, u32[]{:S(2)}) collective-permute-start(bf16[48,768]{1,0:T(8,128)(2,1)S(1)} %bitcast.76), channel_id=1, source_target_pairs={{1,0},{5,1},{9,2},{13,3},{2,4},{6,5},{10,6},{14,7},{3,8},{7,9},{11... | collective-permute-start | bytes 221192 | tf_op jit(solution)/shard_map/ppermute | solution.py:441
  30.4 34.8 %collective-permute-start = (bf16[48,768]{1,0:T(8,128)(2,1)S(1)}, bf16[48,768]{1,0:T(8,128)(2,1)S(1)}, u32[]{:S(2)}, u32[]{:S(2)}) collective-permute-start(bf16[48,768]{1,0:T(8,128)(2,1)S(1)} %bitcast.77), channel_id=1, source_target_pairs={{0,0},{4,1},{8,2},{12,3},{1,4},{5,5},{9,6},{13,7},{2,8},{6,9},{10,... | collective-permute-start | bytes 221192 | tf_op jit(solution)/shard_map/ppermute | solution.py:441
  32.7 32.5 %all-to-all-start.1 = ((bf16[4,48,768]{2,1,0:T(8,128)(2,1)}), bf16[4,48,768]{2,1,0:T(8,128)(2,1)S(1)}, u32[]{:S(2)}, u32[]{:S(2)}) async-start(bf16[4,48,768]{2,1,0:T(8,128)(2,1)} %reshape.298), calls=%async_computation.1 | async-start | bytes 589824 | tf_op jit(solution)/shard_map/all_to_all | solution.py:455
  38.2 85.8 %all-gather.7.cloned.1.call-start = ((), (), s32[]{:S(2)}) async-start(), calls=%async_computation.9 | async-start | bytes 1474560 | tf_op jit(solution)/shard_map/all_gather | solution.py:456
  66.0 135.6 %reduce-scatter.5.cloned.1.call-start = ((), (), s32[]{:S(2)}) async-start(), calls=%async_computation.10 | async-start | bytes 1474560 | tf_op jit(solution)/shard_map/reduce_scatter | solution.py:526
  82.9 24.1 %copy-start.9 = (f32[1024,128]{1,0:T(8,128)}, f32[1024,128]{1,0:T(8,128)S(1)}, u32[]{:S(2)}) copy-start(f32[1024,128]{1,0:T(8,128)S(1)} %get-tuple-element.53.logsum) | copy-start | bytes 1572868
  82.9 1.6 copy-start.6
  138.8 62.9 %reduce-scatter.7.cloned.1.call-start = ((), (), s32[]{:S(2)}) async-start(), calls=%async_computation.11 | async-start | bytes 1474560 | tf_op jit(solution)/shard_map/reduce_scatter | solution.py:527
  139.4 81.4 %reduce-scatter.11.cloned.1.call-start = ((), (), s32[]{:S(2)}) async-start(), calls=%async_computation.13 | async-start | bytes 368640 | tf_op jit(solution)/shard_map/reduce_scatter | solution.py:542
  139.4 1.4 copy-start.15
  166.5 1.3 copy-start.8
  186.0 1.4 copy-start.14
  188.6 13.1 %copy-start.21 = (f32[256,768]{1,0:T(8,128)S(1)}, f32[256,768]{1,0:T(8,128)}, u32[]{:S(2)}) copy-start(f32[256,768]{1,0:T(8,128)} %copy-done.20) | copy-start | bytes 2359300
  201.6 51.0 %reduce-scatter.9.cloned.1.call-start = ((), (), s32[]{:S(2)}) async-start(), calls=%async_computation.12 | async-start | bytes 1638400 | tf_op jit(solution)/shard_map/reduce_scatter | solution.py:559
  201.7 1.4 copy-start.11
  216.1 7.6 %copy-start.24 = (bf16[192,768]{1,0:T(8,128)(2,1)S(1)}, bf16[192,768]{1,0:T(8,128)(2,1)}, u32[]{:S(2)}) copy-start(bf16[192,768]{1,0:T(8,128)(2,1)} %reduce-scatter.5.cloned.1.call-done) | copy-start | bytes 884740
  220.7 1.5 collective-permute-start.6
  222.3 11.5 %collective-permute-start.7 = (bf16[48,768]{1,0:T(8,128)(2,1)S(1)}, bf16[48,768]{1,0:T(8,128)(2,1)S(1)}, u32[]{:S(2)}, u32[]{:S(2)}) collective-permute-start(bf16[48,768]{1,0:T(8,128)(2,1)S(1)} %collective-permute-done.6), channel_id=1, source_target_pairs={{0,16},{16,0},{1,17},{17,1},{2,18},{18,2},{3,19},{19,3},{4,20},{20... | collective-permute-start | bytes 221192 | tf_op jit(solution)/shard_map/ppermute | solution.py:381
  223.7 32.3 %collective-permute-start.9 = (bf16[192,768]{1,0:T(8,128)(2,1)S(1)}, bf16[192,768]{1,0:T(8,128)(2,1)S(1)}, u32[]{:S(2)}, u32[]{:S(2)}) collective-permute-start(bf16[192,768]{1,0:T(8,128)(2,1)S(1)} %copy-done.24), channel_id=1, source_target_pairs={{0,16},{16,0},{1,17},{17,1},{2,18},{18,2},{3,19},{19,3},{4,20},{20... | collective-permute-start | bytes 884744 | tf_op jit(solution)/shard_map/ppermute | solution.py:381
  224.3 15.9 %all-to-all-start.3 = ((bf16[4,48,768]{2,1,0:T(8,128)(2,1)}), bf16[4,48,768]{2,1,0:T(8,128)(2,1)S(1)}, u32[]{:S(2)}, u32[]{:S(2)}) async-start(bf16[4,48,768]{2,1,0:T(8,128)(2,1)} %bitcast.27), calls=%async_computation.7 | async-start | bytes 589824 | tf_op jit(solution)/shard_map/all_to_all | solution.py:539
  241.3 23.0 %collective-permute-start.8 = (bf16[48,3072]{1,0:T(8,128)(2,1)S(1)}, bf16[48,3072]{1,0:T(8,128)(2,1)S(1)}, u32[]{:S(2)}, u32[]{:S(2)}) collective-permute-start(bf16[48,3072]{1,0:T(8,128)(2,1)S(1)} %reshape.308), channel_id=1, source_target_pairs={{0,16},{16,0},{1,17},{17,1},{2,18},{18,2},{3,19},{19,3},{4,20},{20... | collective-permute-start | bytes 884744 | tf_op jit(solution)/shard_map/ppermute | solution.py:381
  252.5 10.2 %all-to-all-start.2 = ((bf16[4,64,576]{2,1,0:T(8,128)(2,1)}), bf16[4,64,576]{2,1,0:T(8,128)(2,1)S(1)}, u32[]{:S(2)}, u32[]{:S(2)}) async-start(bf16[4,64,576]{2,1,0:T(8,128)(2,1)} %reduce-scatter.9.cloned.1.call-done), calls=%async_computation.5 | async-start | bytes 655360 | tf_op jit(solution)/shard_map/all_to_all | solution.py:560
  262.7 3.8 %collective-permute-start.4 = (bf16[1,576]{1,0:T(2,128)(2,1)S(1)}, bf16[1,576]{1,0:T(2,128)(2,1)S(1)}, u32[]{:S(2)}, u32[]{:S(2)}) collective-permute-start(bf16[1,576]{1,0:T(2,128)(2,1)S(1)} %convert_element_type.88), channel_id=1, source_target_pairs={{0,16},{16,0},{1,17},{17,1},{2,18},{18,2},{3,19},{19,3},{4,20},{20... | collective-permute-start | bytes 3464 | tf_op jit(solution)/shard_map/ppermute | solution.py:381
  265.9 6.8 %collective-permute-start.5 = (bf16[48,2304]{1,0:T(8,128)(2,1)S(1)}, bf16[48,2304]{1,0:T(8,128)(2,1)S(1)}, u32[]{:S(2)}, u32[]{:S(2)}) collective-permute-start(bf16[48,2304]{1,0:T(8,128)(2,1)S(1)} %reshape.305), channel_id=1, source_target_pairs={{0,16},{16,0},{1,17},{17,1},{2,18},{18,2},{3,19},{19,3},{4,20},{20... | collective-permute-start | bytes 663560 | tf_op jit(solution)/shard_map/ppermute | solution.py:381
  (14 other events, 15.3 us)
Sparse Core Ops, SparseCore 0:
  25.5 35.8 all-gather.4
  62.9 28.8 all-gather.8
  93.9 29.9 all-gather.6
  138.9 28.2 reduce-scatter.4
  169.4 27.8 reduce-scatter.6
  201.7 18.9 reduce-scatter.10
  223.0 29.4 reduce-scatter.8
